TPU v7x, 512 devices: a whole 4x4x16 slice. The times are simulated.
512 devices in a mesh: section: 2 (over core), grp: 128 (over y_lo, z, x), sub: 2 (over y_hi).
Axes of the slice: x: 4, y: 4 (y_hi: 2, y_lo: 2; y = y_hi * 2 + y_lo), z: 16, core: 2. Of those that a mesh axis runs over, the one named last changes fastest.
Arguments:
- phases: bfloat16 [600, 128, 8192], P(None, 'grp', ('section', 'sub')), may hold values from -8 to 8
- incidence: int32 [600, 2], replicated, may hold values from 0 to 255, as said below
- coherent: int32 [128, 8192], P('grp', ('section', 'sub')), may hold values 0 or 1
Outputs:
- corrected: bfloat16 [256, 128, 8192], P(None, 'grp', ('section', 'sub'))
- trend_fit: float32 [2, 128, 8192], P(None, 'grp', ('section', 'sub'))
Inputs may be any that keep to these rules, and one draw needn't show every extreme that they name: `incidence`: row m holds the primary date and a later secondary date of interferogram m, 1 to 6 dates apart.
All inputs are finite; a program needn't handle non-finite values. No bound on the sum of `coherent` on one device may be relied on, other than what follows from the above.
Results may differ from a plain program's by a relative error of at most 0.0064.
Values may be sent and summed in bfloat16 or wider, within the bound.
A program may use at most 64 MiB of HBM per device.

v0:
```python
import functools
import math

import jax
import jax.numpy as jnp
import numpy as np
from jax import lax
from jax.experimental import pallas as pl
from jax.experimental.pallas import tpu as pltpu
from jax.sharding import PartitionSpec as P

MESH = pl.DeviceIdType.MESH
HIGHEST = lax.Precision.HIGHEST
F32 = jnp.float32
BF16 = jnp.bfloat16

REG = 0.1
FREQS = 256
DATES = 256
ROWS = 128
COLS = 8192
BLOCKS = DATES // 8
COL_DEV = 2048
TILE = 512

PLANE = 32
DEPTH = 16
SHELF = 8


def angle_tables():
    frequency = np.arange(FREQS, dtype=np.int64)[:, None]
    column = np.arange(128, dtype=np.int64)[None, :]
    start = (frequency * column % COLS) * (2.0 * math.pi / COLS)
    step = (frequency * np.full_like(column, 128) % COLS) * (2.0 * math.pi / COLS)
    return np.stack([np.cos(start), np.sin(start), np.cos(step), np.sin(step)]).astype(np.float32)


def row_filter():
    indices = np.arange(ROWS)
    frequency = np.minimum(indices, ROWS - indices).astype(np.float64)
    taper = np.exp(-np.square(frequency / (ROWS / 4.0)))
    turns = (indices[:, None] * indices[None, :] % ROWS) * (2.0 * math.pi / ROWS)
    cos_rows, sin_rows = np.cos(turns), np.sin(turns)
    return ((cos_rows * taper) @ cos_rows.T + (sin_rows * taper) @ sin_rows.T) / ROWS


def smoothing_matrix():
    index = np.arange(DEPTH * SHELF * 2)
    z, shelf, half = index // 16, index // 2 % 8, index % 2
    row = shelf // 4 * 64 + z * 4 + shelf % 4
    full = row_filter()[row[:, None], row[None, :]] * (half[:, None] == half[None, :])
    return full.astype(np.float32)


def column_scales():
    frequency = np.arange(FREQS)
    scale = np.where(frequency == 0, 1.0, 2.0) * np.exp(-np.square(frequency / FREQS)) / COLS
    return scale.astype(np.float32).reshape(2, 1, 128)


def iota(shape, axis):
    return lax.broadcasted_iota(jnp.int32, shape, axis)


def hot(condition):
    return jnp.where(condition, 1.0, 0.0).astype(F32)


def dot(a, b, precision=None):
    return jnp.dot(a, b, precision=precision, preferred_element_type=F32)


def dot_nt(a, b, precision=None):
    return lax.dot_general(
        a, b, (((1,), (1,)), ((), ())), precision=precision, preferred_element_type=F32
    )


def lane_roll(x, shift):
    flat = x.reshape(64, 128)
    return pltpu.roll(flat, shift, 1).reshape(8, 8, 128)


def block_product(a, b):
    total = a[:, 0:1, :] * b[0][None]
    for k in range(1, 8):
        total = total + a[:, k : k + 1, :] * b[k][None]
    return total


def block_inverse(d):
    sub = iota((8, 128), 0)
    rows = [d[i] for i in range(8)]
    for k in range(8):
        pivot = 1.0 / rows[k][k : k + 1, :]
        pivot_row = jnp.where(sub == k, pivot, rows[k] * pivot)
        for i in range(8):
            if i != k:
                factor = rows[i][k : k + 1, :]
                rows[i] = jnp.where(sub == k, 0.0, rows[i]) - factor * pivot_row
        rows[k] = pivot_row
    return jnp.stack(rows)


def pseudo_inverse(incidence):
    count = incidence.shape[1]
    primary, secondary = incidence[0:1, :], incidence[1:2, :]
    dates = iota((DATES, count), 0)
    design_t = hot(dates == secondary) - hot(dates == primary)
    p_in, p_block, s_in, s_block = primary & 7, primary >> 3, secondary & 7, secondary >> 3
    block = iota((128, count), 0) & (BLOCKS - 1)
    at_primary = hot(block == p_block).astype(BF16)
    at_secondary = hot(block == s_block).astype(BF16)
    pair = iota((64, count), 0)
    same = hot(p_block == s_block)
    ps = hot(pair == p_in * 8 + s_in)
    sp = hot(pair == s_in * 8 + p_in)
    on_primary = hot(pair == p_in * 9) - same * (ps + sp)
    on_secondary = hot(pair == s_in * 9)
    to_next = (same - 1.0) * ps
    to_last = (same - 1.0) * sp
    from_primary = dot_nt(jnp.concatenate([on_primary, to_next], 0).astype(BF16), at_primary)
    from_secondary = dot_nt(jnp.concatenate([on_secondary, to_last], 0).astype(BF16), at_secondary)
    entry = iota((64, 128), 0)
    eye = hot((entry >> 3) == (entry & 7))
    diag = (from_primary[:64] + from_secondary[:64] + REG * eye).reshape(8, 8, 128)
    below = from_secondary[64:].reshape(8, 8, 128)
    above = from_primary[64:].reshape(8, 8, 128)
    first = (iota((8, 8, 128), 2) & BLOCKS) == 0

    date = iota((DATES, 128), 0)
    lane = iota((DATES, 128), 1)
    take_first = hot((date >> 3) == lane)
    take_second = hot((date >> 3) == lane - BLOCKS)
    own_row = (iota((DATES, 64), 1) >> 3) == (iota((DATES, 64), 0) & 7)
    spread = hot((iota((64, DATES), 1) & 7) == (iota((64, DATES), 0) & 7))
    row_block = iota((DATES, DATES), 0) >> 3
    col_block = iota((DATES, DATES), 1) >> 3

    def dense(take, x, shift):
        rows = jnp.where(own_row, dot_nt(take, x.reshape(64, 128), HIGHEST), 0.0)
        return jnp.where(col_block == row_block + shift, dot(rows, spread, HIGHEST), 0.0)

    total = None
    step = 1
    while step < BLOCKS:
        inverse = block_inverse(diag)
        near = jnp.where(first, lane_roll(inverse, step), lane_roll(inverse, 128 - step))
        gain = block_product(jnp.where(first, below, above), near)
        back = jnp.where(first, lane_roll(above, step), lane_roll(below, 128 - step))
        change = block_product(gain, back)
        diag = diag - change - lane_roll(change, BLOCKS)
        gamma = dense(take_first, gain, -step) + dense(take_second, gain, step)
        if total is None:
            total = hot(iota((DATES, DATES), 0) == iota((DATES, DATES), 1)) - gamma
        else:
            total = total - dot(gamma, total, HIGHEST)
        if 2 * step < BLOCKS:
            far = jnp.where(first, lane_roll(below, step), lane_roll(above, 128 - step))
            links = -block_product(gain, far)
            swapped = lane_roll(links, BLOCKS)
            below = jnp.where(first, links, swapped)
            above = jnp.where(first, swapped, links)
        step *= 2
    final = dense(take_first, block_inverse(diag), 0)
    return dot(dot(final, total, HIGHEST), design_t, HIGHEST).astype(BF16)


def part_index():
    return lax.axis_index("section") * 2 + lax.axis_index("sub")


def fill_table(angles_ref, table_ref):
    @pl.loop(0, FREQS // 16)
    def _(group):
        first = pl.multiple_of(group * 16, 16)
        rows, sin_rows = pl.ds(first, 16), pl.ds(first + FREQS, 16)
        cos, sin = angles_ref[0, rows, :], angles_ref[1, rows, :]
        step_cos, step_sin = angles_ref[2, rows, :], angles_ref[3, rows, :]
        quarter = ((iota((16, 128), 0) + first) * part_index()) & 3
        odd, minus = (quarter & 1) == 1, quarter >= 2
        cos, sin = jnp.where(odd, -sin, cos), jnp.where(odd, cos, sin)
        cos, sin = jnp.where(minus, -cos, cos), jnp.where(minus, -sin, sin)
        for tile in range(COL_DEV // 128):
            cols = slice(tile * 128, tile * 128 + 128)
            table_ref[rows, cols] = cos.astype(BF16)
            table_ref[sin_rows, cols] = (-sin).astype(BF16)
            cos, sin = cos * step_cos - sin * step_sin, sin * step_cos + cos * step_sin


def regroup_matrix(inverse):
    out, source = iota((256, 256), 0), iota((256, 256), 1)
    if inverse:
        out, source = source, out
    return hot(source == ((out >> 1) & 7) * 32 + (out >> 4) * 2 + (out & 1)).astype(BF16)


def series_kernel(
    incidence_ref,
    coherent_ref,
    angles_ref,
    phases_hbm,
    series_ref,
    trend_ref,
    spectrum_ref,
    table_ref,
    phases_ref,
    map_ref,
    total_ref,
    sem,
):
    load_phases = pltpu.make_async_copy(phases_hbm, phases_ref, sem)
    load_phases.start()
    fill_table(angles_ref, table_ref)
    map_ref[...] = pseudo_inverse(incidence_ref[...])
    total_ref[...] = jnp.zeros_like(total_ref)
    load_phases.wait()
    epochs = (2.0 * iota((DATES, 1), 0).astype(F32) - (DATES - 1)) / (DATES - 1)
    spread = sum(((2.0 * n - (DATES - 1)) / (DATES - 1)) ** 2 for n in range(DATES))

    @pl.loop(0, COL_DEV // TILE)
    def _(tile):
        cols = pl.ds(pl.multiple_of(tile * TILE, TILE), TILE)
        series = dot(map_ref[...], phases_ref[:, cols])
        series_ref[:, cols] = series
        offset = jnp.sum(series, axis=0, keepdims=True) / DATES
        rate = jnp.sum(epochs * series, axis=0, keepdims=True) / spread
        trend_ref[0, :, cols] = offset
        trend_ref[1, :, cols] = rate
        live = coherent_ref[:, cols].astype(F32)
        residual = (live * (series - offset - epochs * rate)).astype(BF16)
        total_ref[...] += dot_nt(residual, table_ref[:, cols])

    for nb in range(8):
        for jb in range(4):
            spectrum_ref[nb * 4 + jb] = total_ref[
                nb * 32 : nb * 32 + 32, jb * 128 : jb * 128 + 128
            ].astype(BF16)


def exchange_kernel(
    spectrum_ref,
    smooth_ref,
    scale_ref,
    weights_ref,
    part_in,
    up_out,
    up_in,
    down_out,
    down_in,
    part_out,
    back_in,
    send_a,
    recv_a,
    send_b,
    recv_b,
    send_c,
    recv_c,
    send_d,
    recv_d,
):
    section, grp, sub = (lax.axis_index(name) for name in ("section", "grp", "sub"))
    shelf = grp // 64 * 4 + grp % 4
    z = grp // 4 % 16
    me = (section * 2 + sub) * 8 + shelf

    def in_plane(other):
        return (
            other // 16,
            other // 4 % 2 * 64 + z * 4 + other % 4,
            other // 8 % 2,
        )

    def along_z(other):
        return (section, grp // 64 * 64 + other * 4 + grp % 4, sub)

    barrier = pltpu.get_barrier_semaphore()

    @pl.loop(1, PLANE)
    def _(hop):
        pl.semaphore_signal(
            barrier, inc=1, device_id=in_plane((me + hop) % PLANE), device_id_type=MESH
        )

    @pl.loop(1, DEPTH)
    def _(hop):
        pl.semaphore_signal(
            barrier, inc=1, device_id=along_z((z + hop) % DEPTH), device_id_type=MESH
        )

    pl.semaphore_wait(barrier, PLANE - 1 + DEPTH - 1)

    def gather(size, mine, source, target, send, recv, where):
        def copy(other, slot, held):
            return pltpu.make_async_remote_copy(
                src_ref=source(other),
                dst_ref=target.at[slot],
                send_sem=send.at[held],
                recv_sem=recv.at[slot],
                device_id=where(other),
                device_id_type=MESH,
            )

        @pl.loop(1, size)
        def _(hop):
            other = (mine + hop) % size
            copy(other, mine, other).start()

        target[mine] = source(mine)[...]

        @pl.loop(1, size)
        def _(hop):
            other = (mine + hop) % size
            copy(other, other, other).wait_recv()

        def finish():
            @pl.loop(1, size)
            def _(hop):
                other = (mine + hop) % size
                copy(other, mine, other).wait_send()

        return finish

    done_a = gather(
        PLANE, me, lambda o: spectrum_ref.at[o], part_in, send_a, recv_a, in_plane
    )
    row_sum = jnp.sum(part_in[...].astype(F32).reshape(4, 256, 128), axis=0).astype(BF16)
    up_out[...] = dot(regroup_matrix(False), row_sum).astype(BF16).reshape(DEPTH, 16, 128)
    done_b = gather(DEPTH, z, lambda o: up_out.at[o], up_in, send_b, recv_b, along_z)
    rows = up_in[...].reshape(256, 128)
    smooth = smooth_ref[...]
    smooth_high = smooth.astype(BF16)
    smooth_low = (smooth - smooth_high.astype(F32)).astype(BF16)
    smoothed = dot(smooth_high, rows) + dot(smooth_low, rows)
    weights = (smoothed * scale_ref[me % 2]).astype(BF16)
    down_out[...] = weights.reshape(DEPTH, 16, 128)
    done_c = gather(DEPTH, z, lambda o: down_out.at[o], down_in, send_c, recv_c, along_z)
    whole = down_in[...].reshape(256, 128)
    part_out[...] = dot(regroup_matrix(True), whole).astype(BF16).reshape(SHELF, 32, 128)
    done_d = gather(
        PLANE, me, lambda o: part_out.at[o % SHELF], back_in, send_d, recv_d, in_plane
    )
    weights_ref[...] = back_in[...]
    done_a()
    done_b()
    done_c()
    done_d()


def correct_kernel(
    coherent_ref, series_ref, weights_ref, table_ref, corrected_ref, flat_ref
):
    for nb in range(8):
        for jb in range(4):
            flat_ref[nb * 32 : nb * 32 + 32, jb * 128 : jb * 128 + 128] = weights_ref[nb * 4 + jb]

    @pl.loop(0, COL_DEV // TILE)
    def _(tile):
        cols = pl.ds(pl.multiple_of(tile * TILE, TILE), TILE)
        screen = dot(flat_ref[...], table_ref[:, cols]).astype(BF16).astype(F32)
        live = coherent_ref[:, cols].astype(F32)
        corrected_ref[:, cols] = (live * (series_ref[:, cols] - screen)).astype(BF16)


def vmem(count):
    return [pl.BlockSpec(memory_space=pltpu.VMEM)] * count


def anywhere(count):
    return [pl.BlockSpec(memory_space=pl.ANY)] * count


def per_device(phases, incidence, coherent):
    ifgs = phases.shape[0]

    series, trend_fit, spectrum, table = pl.pallas_call(
        series_kernel,
        out_shape=(
            jax.ShapeDtypeStruct((DATES, COL_DEV), F32),
            jax.ShapeDtypeStruct((2, 1, COL_DEV), F32),
            jax.ShapeDtypeStruct((PLANE, 32, 128), BF16),
            jax.ShapeDtypeStruct((2 * FREQS, COL_DEV), BF16),
        ),
        in_specs=vmem(3) + anywhere(1),
        out_specs=tuple(vmem(4)),
        scratch_shapes=[
            pltpu.VMEM((ifgs, COL_DEV), BF16),
            pltpu.VMEM((DATES, ifgs), BF16),
            pltpu.VMEM((DATES, 2 * FREQS), F32),
            pltpu.SemaphoreType.DMA,
        ],
        compiler_params=pltpu.CompilerParams(vmem_limit_bytes=40 * 2**20),
        name="series",
    )(incidence.T, coherent, jnp.asarray(angle_tables()), phases.reshape(ifgs, COL_DEV))

    weights = pl.pallas_call(
        exchange_kernel,
        out_shape=jax.ShapeDtypeStruct((PLANE, 32, 128), BF16),
        in_specs=vmem(3),
        out_specs=vmem(1)[0],
        scratch_shapes=[
            pltpu.VMEM((PLANE, 32, 128), BF16),
            pltpu.VMEM((DEPTH, 16, 128), BF16),
            pltpu.VMEM((DEPTH, 16, 128), BF16),
            pltpu.VMEM((DEPTH, 16, 128), BF16),
            pltpu.VMEM((DEPTH, 16, 128), BF16),
            pltpu.VMEM((SHELF, 32, 128), BF16),
            pltpu.VMEM((PLANE, 32, 128), BF16),
        ]
        + [
            pltpu.SemaphoreType.DMA((size,))
            for size in (PLANE, PLANE, DEPTH, DEPTH, DEPTH, DEPTH, PLANE, PLANE)
        ],
        compiler_params=pltpu.CompilerParams(
            collective_id=0, has_side_effects=True, vmem_limit_bytes=32 * 2**20
        ),
        name="exchange",
    )(
        spectrum,
        jnp.asarray(smoothing_matrix()),
        jnp.asarray(column_scales()),
    )

    corrected = pl.pallas_call(
        correct_kernel,
        out_shape=jax.ShapeDtypeStruct((DATES, COL_DEV), BF16),
        in_specs=vmem(4),
        out_specs=vmem(1)[0],
        scratch_shapes=[pltpu.VMEM((DATES, 2 * FREQS), BF16)],
        compiler_params=pltpu.CompilerParams(vmem_limit_bytes=40 * 2**20),
        name="correct",
    )(coherent, series, weights, table)

    return (corrected.reshape(DATES, 1, COL_DEV), trend_fit)


def solution(mesh):
    placed = (P(None, "grp", ("section", "sub")), P(), P("grp", ("section", "sub")))
    return jax.shard_map(
        per_device,
        mesh=mesh,
        in_specs=placed,
        out_specs=(P(None, "grp", ("section", "sub")), P(None, "grp", ("section", "sub"))),
        check_vma=False,
    )
```

profile of v0, /device:TPU:1, one launch (start us, length us, event | category | flops | bytes accessed | tf_op | source)
XLA Modules:
  0.0 69.7 jit_solution(1937638759013663495)
XLA Ops:
  0.6 0.0 copy-start.6
  0.6 0.0 copy-start
  0.7 1.7 %copy-done = bf16[600,1,2048]{2,0,1:T(8,128)(2,1)S(1)} copy-done((bf16[600,1,2048]{2,0,1:T(8,128)(2,1)S(1)}, bf16[600,1,2048]{2,0,1:T(8,128)(2,1)}, u32[]{:S(2)}) %copy-start) | copy-done | bytes 2457624
  2.3 0.0 copy-start.1
  2.3 1.0 %copy-done.1 = f32[4,256,128]{2,1,0:T(8,128)S(1)} copy-done((f32[4,256,128]{2,1,0:T(8,128)S(1)}, f32[4,256,128]{2,1,0:T(8,128)}, u32[]{:S(2)}) %copy-start.1) | copy-done | bytes 524312
  3.4 0.0 copy-start.3
  3.4 0.7 copy-done.3
  4.1 0.0 copy-start.5
  4.1 0.7 copy-done.5
  4.8 0.0 copy-start.2
  4.8 0.0 copy-start.4
  4.8 12.4 %series.1 = (f32[256,2048]{1,0:T(8,128)S(1)}, f32[2,1,2048]{2,1,0:T(1,128)}, bf16[32,32,128]{2,1,0:T(8,128)(2,1)S(1)}, bf16[512,2048]{1,0:T(8,128)(2,1)S(1)}) custom-call(s32[2,600]{1,0:T(2,128)S(1)} %bitcast.4, s32[1,2048]{1,0:T(1,128)S(1)} %copy-done.3, f32[4,256,128]{2,1,0:T(8,128)S(1)} %copy-done.1, bf16[600,2048]{1,0:T(8,128)(2,1)S(1)} %bitcast.3), custom_call_target="tpu_custom_call" | custom-call | tf_op jit(solution)/shard_map/series/pallas_call | solution.py:377
  17.2 0.0 copy-done.6
  17.2 0.0 copy-done.2
  17.2 50.2 %exchange.1.weights_ref = bf16[32,32,128]{2,1,0:T(8,128)(2,1)S(1)} custom-call(bf16[32,32,128]{2,1,0:T(8,128)(2,1)S(1)} %get-tuple-element.7.spectrum_ref, f32[256,256]{1,0:T(8,128)S(1)} %copy-done.2, f32[2,1,128]{2,1,0:T(1,128)S(1)} %copy-done.6), custom_call_target="tpu_custom_call" | custom-call | tf_op jit(solution)/shard_map/exchange/pallas_call | solution.py:397
  67.5 0.0 copy-done.4
  67.5 2.2 %correct.1 = bf16[256,2048]{1,0:T(8,128)(2,1)} custom-call(s32[1,2048]{1,0:T(1,128)S(1)} %copy-done.4, f32[256,2048]{1,0:T(8,128)S(1)} %get-tuple-element.6.series_ref, bf16[32,32,128]{2,1,0:T(8,128)(2,1)S(1)} %exchange.1.weights_ref, bf16[512,2048]{1,0:T(8,128)(2,1)S(1)} %get-tuple-element.8.table_ref), custom_call_target="tpu_custom_call" | custom-call | tf_op jit(solution)/shard_map/correct/pallas_call | solution.py:425
Async XLA Ops:
  0.6 16.6 %copy-start.6 = (f32[2,1,128]{2,1,0:T(1,128)S(1)}, f32[2,1,128]{2,1,0:T(1,128)}, u32[]{:S(2)}) copy-start(f32[2,1,128]{2,1,0:T(1,128)} %constant.8.clone.scale_ref) | copy-start | bytes 3076
  0.6 1.7 %copy-start = (bf16[600,1,2048]{2,0,1:T(8,128)(2,1)S(1)}, bf16[600,1,2048]{2,0,1:T(8,128)(2,1)}, u32[]{:S(2)}) copy-start(bf16[600,1,2048]{2,0,1:T(8,128)(2,1)} %param.6) | copy-start | bytes 7372804
  2.3 1.0 %copy-start.1 = (f32[4,256,128]{2,1,0:T(8,128)S(1)}, f32[4,256,128]{2,1,0:T(8,128)}, u32[]{:S(2)}) copy-start(f32[4,256,128]{2,1,0:T(8,128)} %constant.6.clone.angles_ref) | copy-start | bytes 1572868
  3.4 0.7 copy-start.3
  4.1 0.7 copy-start.5
  4.8 12.5 %copy-start.2 = (f32[256,256]{1,0:T(8,128)S(1)}, f32[256,256]{1,0:T(8,128)}, u32[]{:S(2)}) copy-start(f32[256,256]{1,0:T(8,128)} %constant.7.clone.smooth_ref) | copy-start | bytes 786436
  4.8 62.7 %copy-start.4 = (s32[1,2048]{1,0:T(1,128)S(1)}, s32[1,2048]{1,0:T(1,128)}, u32[]{:S(2)}) copy-start(s32[1,2048]{1,0:T(1,128)} %coherent_ref.3) | copy-start | bytes 24580
where the time goes:
time: 70 us; the launch traced here: 69.7 us
  Pallas kernels  64.9 us (93%)
  local copies, waits for them, and re-layouts  4.13 us (6%)
    pallas_call x1, Pallas kernels, per_device(): pl.pallas_call(exchange_kernel, out_shape=jax.ShapeDtypeStruct((PLANE, 32...  50.2 us
    pallas_call x1, Pallas kernels, per_device(): pl.pallas_call(series_kernel, out_shape=(jax.ShapeDtypeStruct((DATES, COL...  12.4 us
    unnamed x14, local copies, waits for them, and re-layouts  4.13 us
    pallas_call x1, Pallas kernels, per_device(): pl.pallas_call(correct_kernel, out_shape=jax.ShapeDtypeStruct((DATES, COL...  2.25 us

commit v1 on v0

v1 whole, which is shorter than its diff:
```python
import math

import jax
import jax.numpy as jnp
import numpy as np
from jax import lax
from jax.experimental import pallas as pl
from jax.experimental.pallas import tpu as pltpu
from jax.sharding import PartitionSpec as P

MESH = pl.DeviceIdType.MESH
F32 = jnp.float32
BF16 = jnp.bfloat16

REG = 0.1
FREQS = 256
DATES = 256
ROWS = 128
COLS = 8192
BLOCKS = DATES // 8
COL_DEV = 2048
TILE = 512

PLANE = 32
DEPTH = 16
SHELF = 8


def angle_tables():
    frequency = np.arange(FREQS, dtype=np.int64)[:, None]
    column = np.arange(128, dtype=np.int64)[None, :]
    start = (frequency * column % COLS) * (2.0 * math.pi / COLS)
    step = (frequency * np.full_like(column, 128) % COLS) * (2.0 * math.pi / COLS)
    return np.stack([np.cos(start), np.sin(start), np.cos(step), np.sin(step)]).astype(np.float32)


def row_filter():
    indices = np.arange(ROWS)
    frequency = np.minimum(indices, ROWS - indices).astype(np.float64)
    taper = np.exp(-np.square(frequency / (ROWS / 4.0)))
    turns = (indices[:, None] * indices[None, :] % ROWS) * (2.0 * math.pi / ROWS)
    cos_rows, sin_rows = np.cos(turns), np.sin(turns)
    return ((cos_rows * taper) @ cos_rows.T + (sin_rows * taper) @ sin_rows.T) / ROWS


def smoothing_matrix():
    index = np.arange(DEPTH * SHELF * 2)
    z, shelf, half = index // 16, index // 2 % 8, index % 2
    row = shelf // 4 * 64 + z * 4 + shelf % 4
    full = row_filter()[row[:, None], row[None, :]] * (half[:, None] == half[None, :])
    return full.astype(np.float32)


def column_scales():
    frequency = np.arange(FREQS)
    scale = np.where(frequency == 0, 1.0, 2.0) * np.exp(-np.square(frequency / FREQS)) / COLS
    return scale.astype(np.float32).reshape(2, 1, 128)


def iota(shape, axis):
    return lax.broadcasted_iota(jnp.int32, shape, axis)


def hot(condition):
    return jnp.where(condition, 1.0, 0.0).astype(F32)


def dot(a, b):
    return jnp.dot(a, b, preferred_element_type=F32)


def dot_nt(a, b):
    return lax.dot_general(a, b, (((1,), (1,)), ((), ())), preferred_element_type=F32)


def lane_roll(x, shift):
    flat = x.reshape(64, 128)
    return pltpu.roll(flat, shift, 1).reshape(8, 8, 128)


def block_product(a, b):
    total = a[:, 0:1, :] * b[0][None]
    for k in range(1, 8):
        total = total + a[:, k : k + 1, :] * b[k][None]
    return total


def reciprocal(x):
    guess = pl.reciprocal(x, approx=True)
    guess = guess * (2.0 - x * guess)
    return guess * (2.0 - x * guess)


def block_inverse(d):
    sub = iota((8, 128), 0)
    rows = [d[i] for i in range(8)]
    for k in range(8):
        pivot = reciprocal(rows[k][k : k + 1, :])
        pivot_row = jnp.where(sub == k, pivot, rows[k] * pivot)
        for i in range(8):
            if i != k:
                factor = rows[i][k : k + 1, :]
                rows[i] = jnp.where(sub == k, 0.0, rows[i]) - factor * pivot_row
        rows[k] = pivot_row
    return jnp.stack(rows)


def split(x):
    high = x.astype(BF16)
    rest = x - high.astype(F32)
    middle = rest.astype(BF16)
    return high, middle, (rest - middle.astype(F32)).astype(BF16)


def dot_split(a, b):
    (ah, am, al), (bh, bm, bl) = a, b
    return dot(
        jnp.concatenate([al, am, ah, am, ah, ah], axis=1),
        jnp.concatenate([bh, bm, bl, bh, bm, bh], axis=0),
    )


def pseudo_inverse(incidence):
    count = incidence.shape[1]
    primary, secondary = incidence[0:1, :], incidence[1:2, :]
    dates = iota((DATES, count), 0)
    design_t = hot(dates == secondary) - hot(dates == primary)
    p_in, p_block, s_in, s_block = primary & 7, primary >> 3, secondary & 7, secondary >> 3
    block = iota((128, count), 0) & (BLOCKS - 1)
    at_primary = hot(block == p_block).astype(BF16)
    at_secondary = hot(block == s_block).astype(BF16)
    pair = iota((64, count), 0)
    same = hot(p_block == s_block)
    ps = hot(pair == p_in * 8 + s_in)
    sp = hot(pair == s_in * 8 + p_in)
    on_primary = hot(pair == p_in * 9) - same * (ps + sp)
    on_secondary = hot(pair == s_in * 9)
    to_next = (same - 1.0) * ps
    to_last = (same - 1.0) * sp
    from_primary = dot_nt(jnp.concatenate([on_primary, to_next], 0).astype(BF16), at_primary)
    from_secondary = dot_nt(jnp.concatenate([on_secondary, to_last], 0).astype(BF16), at_secondary)
    entry = iota((64, 128), 0)
    eye = hot((entry >> 3) == (entry & 7))
    diag = (from_primary[:64] + from_secondary[:64] + REG * eye).reshape(8, 8, 128)
    below = from_secondary[64:].reshape(8, 8, 128)
    above = from_primary[64:].reshape(8, 8, 128)
    first = (iota((8, 8, 128), 2) & BLOCKS) == 0

    date = iota((2 * DATES, 128), 0)
    take = hot((date >> 3) == iota((2 * DATES, 128), 1)).astype(BF16)
    own_row = ((iota((2 * DATES, 192), 1) >> 3) & 7) == (iota((2 * DATES, 192), 0) & 7)
    spread = hot((iota((192, DATES), 1) & 7) == (iota((192, DATES), 0) & 7)).astype(BF16)
    row_block = iota((DATES, DATES), 0) >> 3
    col_block = iota((DATES, DATES), 1) >> 3

    def blocks_of(x, sides):
        count = sides * DATES
        terms = jnp.concatenate(split(x.reshape(64, 128)), axis=0)
        rows = jnp.where(own_row[:count], dot_nt(take[:count], terms), 0.0).astype(BF16)
        return dot(rows, spread)

    total = None
    step = 1
    while step < BLOCKS:
        inverse = block_inverse(diag)
        near = jnp.where(first, lane_roll(inverse, step), lane_roll(inverse, 128 - step))
        gain = block_product(jnp.where(first, below, above), near)
        back = jnp.where(first, lane_roll(above, step), lane_roll(below, 128 - step))
        change = block_product(gain, back)
        diag = diag - change - lane_roll(change, BLOCKS)
        sides = blocks_of(gain, 2)
        gamma = jnp.where(
            col_block == row_block - step,
            sides[:DATES],
            jnp.where(col_block == row_block + step, sides[DATES:], 0.0),
        )
        if total is None:
            total = hot(iota((DATES, DATES), 0) == iota((DATES, DATES), 1)) - gamma
        else:
            total = total - dot_split(split(gamma), split(total))
        if 2 * step < BLOCKS:
            far = jnp.where(first, lane_roll(below, step), lane_roll(above, 128 - step))
            links = -block_product(gain, far)
            swapped = lane_roll(links, BLOCKS)
            below = jnp.where(first, links, swapped)
            above = jnp.where(first, swapped, links)
        step *= 2
    final = jnp.where(col_block == row_block, blocks_of(block_inverse(diag), 1), 0.0)
    inverse = dot_split(split(final), split(total))
    design_t = design_t.astype(BF16)
    return dot(
        jnp.concatenate(split(inverse)[::-1], axis=1),
        jnp.concatenate([design_t, design_t, design_t], axis=0),
    ).astype(BF16)


def part_index():
    return lax.axis_index("section") * 2 + lax.axis_index("sub")


def fill_table(angles_ref, table_ref):
    @pl.loop(0, FREQS // 16)
    def _(group):
        first = pl.multiple_of(group * 16, 16)
        rows, sin_rows = pl.ds(first, 16), pl.ds(first + FREQS, 16)
        cos, sin = angles_ref[0, rows, :], angles_ref[1, rows, :]
        step_cos, step_sin = angles_ref[2, rows, :], angles_ref[3, rows, :]
        quarter = ((iota((16, 128), 0) + first) * part_index()) & 3
        odd, minus = (quarter & 1) == 1, quarter >= 2
        cos, sin = jnp.where(odd, -sin, cos), jnp.where(odd, cos, sin)
        cos, sin = jnp.where(minus, -cos, cos), jnp.where(minus, -sin, sin)
        for tile in range(COL_DEV // 128):
            cols = slice(tile * 128, tile * 128 + 128)
            table_ref[rows, cols] = cos.astype(BF16)
            table_ref[sin_rows, cols] = (-sin).astype(BF16)
            cos, sin = cos * step_cos - sin * step_sin, sin * step_cos + cos * step_sin


def regroup_matrix(inverse):
    out, source = iota((256, 256), 0), iota((256, 256), 1)
    if inverse:
        out, source = source, out
    return hot(source == ((out >> 1) & 7) * 32 + (out >> 4) * 2 + (out & 1)).astype(BF16)


def screen_kernel(
    incidence_hbm,
    coherent_hbm,
    angles_hbm,
    smooth_hbm,
    scale_hbm,
    phases_hbm,
    corrected_hbm,
    trend_hbm,
    incidence_ref,
    coherent_ref,
    angles_ref,
    smooth_ref,
    scale_ref,
    phases_ref,
    corrected_ref,
    trend_ref,
    table_ref,
    series_ref,
    map_ref,
    total_ref,
    part_out,
    part_in,
    up_out,
    up_in,
    down_out,
    down_in,
    back_out,
    back_in,
    flat_ref,
    load_sems,
    store_sems,
    send_sems,
    recv_sems,
):
    loads = [
        pltpu.make_async_copy(source, target, load_sems.at[i])
        for i, (source, target) in enumerate(
            [
                (incidence_hbm, incidence_ref),
                (angles_hbm, angles_ref),
                (coherent_hbm, coherent_ref),
                (phases_hbm, phases_ref),
                (smooth_hbm, smooth_ref),
                (scale_hbm, scale_ref),
            ]
        )
    ]
    for load in loads:
        load.start()

    section, grp, sub = (lax.axis_index(name) for name in ("section", "grp", "sub"))
    y, z, x = grp // 64, grp // 4 % 16, grp % 4
    me = (section * 2 + sub) * 8 + y * 4 + x
    sections, subs, ys = (section, 1 - section), (sub, 1 - sub), (y, 1 - y)
    xs = [(x + hop) % 4 for hop in range(4)]
    zs = [(z + hop) % 16 for hop in range(16)]
    plane = [
        ((a * 2 + b) * 8 + c * 4 + d, c * 4 + d, (a, c * 64 + z * 4 + d, b))
        for d in xs
        for c in ys
        for b in subs
        for a in sections
    ][1:]
    column = [(other, other, (section, y * 64 + other * 4 + x, sub)) for other in zs][1:]

    barrier = pltpu.get_barrier_semaphore()
    for _, _, device in plane + column:
        pl.semaphore_signal(barrier, inc=1, device_id=device, device_id_type=MESH)

    loads[1].wait()
    fill_table(angles_ref, table_ref)
    loads[0].wait()
    map_ref[...] = pseudo_inverse(incidence_ref[...])
    total_ref[...] = jnp.zeros_like(total_ref)
    epochs = (2.0 * iota((DATES, 1), 0).astype(F32) - (DATES - 1)) / (DATES - 1)
    spread = sum(((2.0 * n - (DATES - 1)) / (DATES - 1)) ** 2 for n in range(DATES))
    for load in loads[2:]:
        load.wait()

    @pl.loop(0, COL_DEV // TILE)
    def _(tile):
        cols = pl.ds(pl.multiple_of(tile * TILE, TILE), TILE)
        series = dot(map_ref[...], phases_ref[:, cols])
        series_ref[:, cols] = series
        offset = jnp.sum(series, axis=0, keepdims=True) / DATES
        rate = jnp.sum(epochs * series, axis=0, keepdims=True) / spread
        trend_ref[0, :, cols] = offset
        trend_ref[1, :, cols] = rate
        live = coherent_ref[:, cols].astype(F32)
        residual = (live * (series - offset - epochs * rate)).astype(BF16)
        total_ref[...] += dot_nt(residual, table_ref[:, cols])

    for nb in range(8):
        for jb in range(4):
            part_out[nb * 4 + jb] = total_ref[
                nb * 32 : nb * 32 + 32, jb * 128 : jb * 128 + 128
            ].astype(BF16)

    trend_store = pltpu.make_async_copy(trend_ref, trend_hbm, store_sems.at[COL_DEV // TILE])
    trend_store.start()
    pl.semaphore_wait(barrier, len(plane) + len(column))

    def exchange(phase, mine, partners, source, target):
        for other, row, device in partners:
            pltpu.make_async_remote_copy(
                src_ref=source(other, row),
                dst_ref=target.at[mine],
                send_sem=send_sems.at[phase],
                recv_sem=recv_sems.at[phase],
                device_id=device,
                device_id_type=MESH,
            ).start()
        target[mine] = source(mine, lax.rem(mine, SHELF))[...]

    def arrived(phase, target, sems):
        blocks = target.at[pl.ds(0, target.shape[0] - 1)]
        pltpu.make_async_copy(blocks, blocks, sems.at[phase]).wait()

    exchange(0, me, plane, lambda other, row: part_out.at[other], part_in)
    smooth = smooth_ref[...]
    smooth_high = smooth.astype(BF16)
    smooth_low = (smooth - smooth_high.astype(F32)).astype(BF16)
    regroup, ungroup = regroup_matrix(False), regroup_matrix(True)
    arrived(0, part_in, recv_sems)
    row_sum = jnp.sum(part_in[...].astype(F32).reshape(4, 256, 128), axis=0).astype(BF16)
    up_out[...] = dot(regroup, row_sum).astype(BF16).reshape(DEPTH, 16, 128)
    exchange(1, z, column, lambda other, row: up_out.at[other], up_in)
    arrived(1, up_in, recv_sems)
    rows = up_in[...].reshape(256, 128)
    smoothed = dot(smooth_high, rows) + dot(smooth_low, rows)
    down_out[...] = (smoothed * scale_ref[me % 2]).astype(BF16).reshape(DEPTH, 16, 128)
    exchange(2, z, column, lambda other, row: down_out.at[other], down_in)
    arrived(2, down_in, recv_sems)
    whole = down_in[...].reshape(256, 128)
    back_out[...] = dot(ungroup, whole).astype(BF16).reshape(SHELF, 32, 128)
    exchange(3, me, plane, lambda other, row: back_out.at[row], back_in)
    arrived(3, back_in, recv_sems)

    for nb in range(8):
        for jb in range(4):
            flat_ref[nb * 32 : nb * 32 + 32, jb * 128 : jb * 128 + 128] = back_in[nb * 4 + jb]

    def store(tile):
        cols = pl.ds(pl.multiple_of(tile * TILE, TILE), TILE)
        return pltpu.make_async_copy(
            corrected_ref.at[:, cols], corrected_hbm.at[:, cols], store_sems.at[tile]
        )

    @pl.loop(0, COL_DEV // TILE)
    def _(tile):
        cols = pl.ds(pl.multiple_of(tile * TILE, TILE), TILE)
        screen = dot(flat_ref[...], table_ref[:, cols]).astype(BF16).astype(F32)
        live = coherent_ref[:, cols].astype(F32)
        corrected_ref[:, cols] = (live * (series_ref[:, cols] - screen)).astype(BF16)
        store(tile).start()

    arrived(0, part_in, send_sems)
    arrived(1, up_in, send_sems)
    arrived(2, down_in, send_sems)
    arrived(3, back_in, send_sems)
    trend_store.wait()

    @pl.loop(0, COL_DEV // TILE)
    def _(tile):
        store(tile).wait()


def per_device(phases, incidence, coherent):
    ifgs = phases.shape[0]
    anywhere = pl.BlockSpec(memory_space=pl.ANY)
    corrected, trend_fit = pl.pallas_call(
        screen_kernel,
        out_shape=(
            jax.ShapeDtypeStruct((DATES, COL_DEV), BF16),
            jax.ShapeDtypeStruct((2, 1, COL_DEV), F32),
        ),
        in_specs=[anywhere] * 6,
        out_specs=(anywhere, anywhere),
        scratch_shapes=[
            pltpu.VMEM((2, ifgs), jnp.int32),
            pltpu.VMEM((1, COL_DEV), jnp.int32),
            pltpu.VMEM((4, FREQS, 128), F32),
            pltpu.VMEM((256, 256), F32),
            pltpu.VMEM((2, 1, 128), F32),
            pltpu.VMEM((ifgs, COL_DEV), BF16),
            pltpu.VMEM((DATES, COL_DEV), BF16),
            pltpu.VMEM((2, 1, COL_DEV), F32),
            pltpu.VMEM((2 * FREQS, COL_DEV), BF16),
            pltpu.VMEM((DATES, COL_DEV), F32),
            pltpu.VMEM((DATES, ifgs), BF16),
            pltpu.VMEM((DATES, 2 * FREQS), F32),
            pltpu.VMEM((PLANE, 32, 128), BF16),
            pltpu.VMEM((PLANE, 32, 128), BF16),
            pltpu.VMEM((DEPTH, 16, 128), BF16),
            pltpu.VMEM((DEPTH, 16, 128), BF16),
            pltpu.VMEM((DEPTH, 16, 128), BF16),
            pltpu.VMEM((DEPTH, 16, 128), BF16),
            pltpu.VMEM((SHELF, 32, 128), BF16),
            pltpu.VMEM((PLANE, 32, 128), BF16),
            pltpu.VMEM((DATES, 2 * FREQS), BF16),
            pltpu.SemaphoreType.DMA((6,)),
            pltpu.SemaphoreType.DMA((COL_DEV // TILE + 1,)),
            pltpu.SemaphoreType.DMA((4,)),
            pltpu.SemaphoreType.DMA((4,)),
        ],
        compiler_params=pltpu.CompilerParams(
            collective_id=0, has_side_effects=True, vmem_limit_bytes=64 * 2**20
        ),
        name="screen",
    )(
        incidence.T,
        coherent,
        jnp.asarray(angle_tables()),
        jnp.asarray(smoothing_matrix()),
        jnp.asarray(column_scales()),
        phases.reshape(ifgs, COL_DEV),
    )
    return (corrected.reshape(DATES, 1, COL_DEV), trend_fit)


def solution(mesh):
    placed = (P(None, "grp", ("section", "sub")), P(), P("grp", ("section", "sub")))
    return jax.shard_map(
        per_device,
        mesh=mesh,
        in_specs=placed,
        out_specs=(P(None, "grp", ("section", "sub")), P(None, "grp", ("section", "sub"))),
        check_vma=False,
    )
```

time: 70 us -> 54.1 us (0.77)
  Pallas kernels: 64.9 us -> 49.6 us
    pallas_call x3 -> x1, Pallas kernels: 64.9 us -> 49.6 us  [per_device(): pl.pallas_call(screen_kernel, out_shape=(jax.ShapeDtypeStruct((DATES, COL...]
    unnamed x14 -> x2, local copies, waits for them, and re-layouts: 4.13 us -> 3.63 us
where the time goes in v1:
time: 54.1 us; the launch traced here: 53.9 us
  Pallas kernels  49.6 us (92%)
  local copies, waits for them, and re-layouts  3.63 us (7%)
  between operations  0.64 us (1%)
    pallas_call x1, Pallas kernels, per_device(): pl.pallas_call(screen_kernel, out_shape=(jax.ShapeDtypeStruct((DATES, COL...  49.6 us
    unnamed x2, local copies, waits for them, and re-layouts  3.63 us

profile of v1, /device:TPU:1, one launch (start us, length us, event | category | flops | bytes accessed | tf_op | source)
XLA Modules:
  0.0 53.9 jit_solution(10273159351325063681)
XLA Ops:
  0.6 49.6 %screen.1 = (bf16[256,2048]{1,0:T(8,128)(2,1)}, f32[2,1,2048]{2,1,0:T(1,128)}) custom-call(s32[2,600]{1,0:T(2,128)} %bitcast.5, s32[1,2048]{1,0:T(1,128)} %coherent_hbm.1, f32[4,256,128]{2,1,0:T(8,128)} %constant.6.clone.angles_hbm, f32[256,256]{1,0:T(8,128)} %constant.7.clone.smooth_hbm, f32[2,1,128]{2,1,0:T(1,128)} %constant.8.clone.scale_hbm, ...), custom_call_target="tpu_custom_call" | custom-call | tf_op jit(solution)/shard_map/screen/pallas_call | solution.py:397
  50.3 2.3 %copy.10 = bf16[256,1,2048]{2,0,1:T(8,128)(2,1)} copy(bf16[256,1,2048]{2,0,1:T(8,128)(2,1)} %bitcast.4) | data formatting | bytes 2097152
  52.6 1.3 %copy.11 = f32[2,1,2048]{2,1,0:T(1,128)} copy(f32[2,1,2048]{2,1,0:T(1,128)} %get-tuple-element.9) | data formatting | bytes 32768

commit v2 on v1

--- a/solution.py
+++ b/solution.py
@@ -21,7 +21,8 @@
 COL_DEV = 2048
 TILE = 512
 
-PLANE = 32
+PLANE = 16
+HALF = DATES // 2
 DEPTH = 16
 SHELF = 8
 
@@ -199,13 +200,13 @@
 
 
 def fill_table(angles_ref, table_ref):
-    @pl.loop(0, FREQS // 16)
+    @pl.loop(0, FREQS // 64)
     def _(group):
-        first = pl.multiple_of(group * 16, 16)
-        rows, sin_rows = pl.ds(first, 16), pl.ds(first + FREQS, 16)
+        first = pl.multiple_of(group * 64, 64)
+        rows, sin_rows = pl.ds(first, 64), pl.ds(first + FREQS, 64)
         cos, sin = angles_ref[0, rows, :], angles_ref[1, rows, :]
         step_cos, step_sin = angles_ref[2, rows, :], angles_ref[3, rows, :]
-        quarter = ((iota((16, 128), 0) + first) * part_index()) & 3
+        quarter = ((iota((64, 128), 0) + first) * part_index()) & 3
         odd, minus = (quarter & 1) == 1, quarter >= 2
         cos, sin = jnp.where(odd, -sin, cos), jnp.where(odd, cos, sin)
         cos, sin = jnp.where(minus, -cos, cos), jnp.where(minus, -sin, sin)
@@ -230,20 +231,20 @@
     smooth_hbm,
     scale_hbm,
     phases_hbm,
-    corrected_hbm,
-    trend_hbm,
+    corrected_ref,
+    trend_ref,
     incidence_ref,
     coherent_ref,
     angles_ref,
     smooth_ref,
     scale_ref,
     phases_ref,
-    corrected_ref,
-    trend_ref,
     table_ref,
     series_ref,
+    residual_ref,
     map_ref,
-    total_ref,
+    pair_out,
+    pair_in,
     part_out,
     part_in,
     up_out,
@@ -252,9 +253,9 @@
     down_in,
     back_out,
     back_in,
+    swap_in,
     flat_ref,
     load_sems,
-    store_sems,
     send_sems,
     recv_sems,
 ):
@@ -276,36 +277,34 @@
 
     section, grp, sub = (lax.axis_index(name) for name in ("section", "grp", "sub"))
     y, z, x = grp // 64, grp // 4 % 16, grp % 4
-    me = (section * 2 + sub) * 8 + y * 4 + x
-    sections, subs, ys = (section, 1 - section), (sub, 1 - sub), (y, 1 - y)
-    xs = [(x + hop) % 4 for hop in range(4)]
-    zs = [(z + hop) % 16 for hop in range(16)]
+    me = sub * 8 + y * 4 + x
+    subs, ys = (sub, 1 - sub), (y, 1 - y)
+    xs = [(x + hop) % 4 for hop in (2, 1, 3, 0)]
+    zs = [(z + hop) % 16 for hop in (8, 7, 9, 6, 10, 5, 11, 4, 12, 3, 13, 2, 14, 1, 15)]
     plane = [
-        ((a * 2 + b) * 8 + c * 4 + d, c * 4 + d, (a, c * 64 + z * 4 + d, b))
+        (b * 8 + c * 4 + d, c * 4 + d, (section, c * 64 + z * 4 + d, b))
         for d in xs
-        for c in ys
-        for b in subs
-        for a in sections
-    ][1:]
-    column = [(other, other, (section, y * 64 + other * 4 + x, sub)) for other in zs][1:]
+        for b in subs[::-1]
+        for c in ys[::-1]
+    ][:-1]
+    column = [(other, other, (section, y * 64 + other * 4 + x, sub)) for other in zs]
+    partner = (1 - section, grp, sub)
 
     barrier = pltpu.get_barrier_semaphore()
-    for _, _, device in plane + column:
+    for device in [partner] + [device for _, _, device in plane + column]:
         pl.semaphore_signal(barrier, inc=1, device_id=device, device_id_type=MESH)
 
     loads[1].wait()
     fill_table(angles_ref, table_ref)
     loads[0].wait()
     map_ref[...] = pseudo_inverse(incidence_ref[...])
-    total_ref[...] = jnp.zeros_like(total_ref)
     epochs = (2.0 * iota((DATES, 1), 0).astype(F32) - (DATES - 1)) / (DATES - 1)
     spread = sum(((2.0 * n - (DATES - 1)) / (DATES - 1)) ** 2 for n in range(DATES))
     for load in loads[2:]:
         load.wait()
 
-    @pl.loop(0, COL_DEV // TILE)
-    def _(tile):
-        cols = pl.ds(pl.multiple_of(tile * TILE, TILE), TILE)
+    for tile in range(COL_DEV // TILE):
+        cols = slice(tile * TILE, tile * TILE + TILE)
         series = dot(map_ref[...], phases_ref[:, cols])
         series_ref[:, cols] = series
         offset = jnp.sum(series, axis=0, keepdims=True) / DATES
@@ -313,18 +312,33 @@
         trend_ref[0, :, cols] = offset
         trend_ref[1, :, cols] = rate
         live = coherent_ref[:, cols].astype(F32)
-        residual = (live * (series - offset - epochs * rate)).astype(BF16)
-        total_ref[...] += dot_nt(residual, table_ref[:, cols])
-
-    for nb in range(8):
-        for jb in range(4):
-            part_out[nb * 4 + jb] = total_ref[
-                nb * 32 : nb * 32 + 32, jb * 128 : jb * 128 + 128
-            ].astype(BF16)
-
-    trend_store = pltpu.make_async_copy(trend_ref, trend_hbm, store_sems.at[COL_DEV // TILE])
-    trend_store.start()
-    pl.semaphore_wait(barrier, len(plane) + len(column))
+        residual_ref[:, cols] = (live * (series - offset - epochs * rate)).astype(BF16)
+
+    def half_rows(half):
+        return pl.ds(pl.multiple_of(half * HALF, HALF), HALF)
+
+    def block(array, number):
+        row, col = number // 4 * 32, number % 4 * 128
+        return array[row : row + 32, col : col + 128]
+
+    pl.semaphore_wait(barrier, 1 + len(plane) + len(column))
+
+    theirs = dot_nt(residual_ref[half_rows(1 - section), :], table_ref[...]).astype(BF16)
+    for number in range(PLANE):
+        pair_out[number] = block(theirs, number)
+    give = pltpu.make_async_remote_copy(
+        src_ref=pair_out,
+        dst_ref=pair_in,
+        send_sem=send_sems.at[4],
+        recv_sem=recv_sems.at[4],
+        device_id=partner,
+        device_id_type=MESH,
+    )
+    give.start()
+    ours = dot_nt(residual_ref[half_rows(section), :], table_ref[...])
+    give.wait_recv()
+    for number in range(PLANE):
+        part_out[number] = (block(ours, number) + pair_in[number].astype(F32)).astype(BF16)
 
     def exchange(phase, mine, partners, source, target):
         for other, row, device in partners:
@@ -348,7 +362,7 @@
     smooth_low = (smooth - smooth_high.astype(F32)).astype(BF16)
     regroup, ungroup = regroup_matrix(False), regroup_matrix(True)
     arrived(0, part_in, recv_sems)
-    row_sum = jnp.sum(part_in[...].astype(F32).reshape(4, 256, 128), axis=0).astype(BF16)
+    row_sum = jnp.sum(part_in[...].astype(F32).reshape(2, 256, 128), axis=0).astype(BF16)
     up_out[...] = dot(regroup, row_sum).astype(BF16).reshape(DEPTH, 16, 128)
     exchange(1, z, column, lambda other, row: up_out.at[other], up_in)
     arrived(1, up_in, recv_sems)
@@ -362,46 +376,70 @@
     exchange(3, me, plane, lambda other, row: back_out.at[row], back_in)
     arrived(3, back_in, recv_sems)
 
-    for nb in range(8):
-        for jb in range(4):
-            flat_ref[nb * 32 : nb * 32 + 32, jb * 128 : jb * 128 + 128] = back_in[nb * 4 + jb]
-
-    def store(tile):
-        cols = pl.ds(pl.multiple_of(tile * TILE, TILE), TILE)
-        return pltpu.make_async_copy(
-            corrected_ref.at[:, cols], corrected_hbm.at[:, cols], store_sems.at[tile]
-        )
-
-    @pl.loop(0, COL_DEV // TILE)
-    def _(tile):
-        cols = pl.ds(pl.multiple_of(tile * TILE, TILE), TILE)
-        screen = dot(flat_ref[...], table_ref[:, cols]).astype(BF16).astype(F32)
-        live = coherent_ref[:, cols].astype(F32)
-        corrected_ref[:, cols] = (live * (series_ref[:, cols] - screen)).astype(BF16)
-        store(tile).start()
-
+    swap = pltpu.make_async_remote_copy(
+        src_ref=back_in,
+        dst_ref=swap_in,
+        send_sem=send_sems.at[5],
+        recv_sem=recv_sems.at[5],
+        device_id=partner,
+        device_id_type=MESH,
+    )
+    swap.start()
+
+    def correct(half, weights):
+        for number in range(PLANE):
+            row, col = number // 4 * 32, number % 4 * 128
+            flat_ref[row : row + 32, col : col + 128] = weights[number]
+        dates = half_rows(half)
+        for tile in range(COL_DEV // TILE):
+            cols = slice(tile * TILE, tile * TILE + TILE)
+            screen = dot(flat_ref[...], table_ref[:, cols]).astype(BF16).astype(F32)
+            live = coherent_ref[:, cols].astype(F32)
+            corrected_ref[dates, cols] = (live * (series_ref[dates, cols] - screen)).astype(BF16)
+
+    correct(section, back_in)
+    give.wait_send()
     arrived(0, part_in, send_sems)
     arrived(1, up_in, send_sems)
     arrived(2, down_in, send_sems)
     arrived(3, back_in, send_sems)
-    trend_store.wait()
-
-    @pl.loop(0, COL_DEV // TILE)
-    def _(tile):
-        store(tile).wait()
+    swap.wait_recv()
+    correct(1 - section, swap_in)
+    swap.wait_send()
+
+
+def store_kernel(corrected_ref, trend_ref, corrected_hbm, trend_hbm, sems):
+    stores = [
+        pltpu.make_async_copy(corrected_ref, corrected_hbm, sems.at[0]),
+        pltpu.make_async_copy(trend_ref, trend_hbm, sems.at[1]),
+    ]
+    for store in stores:
+        store.start()
+    for store in stores:
+        store.wait()
 
 
 def per_device(phases, incidence, coherent):
     ifgs = phases.shape[0]
-    anywhere = pl.BlockSpec(memory_space=pl.ANY)
+    in_hbm = pl.BlockSpec(memory_space=pltpu.HBM)
+    in_vmem = pl.BlockSpec(memory_space=pltpu.VMEM)
+    results = (
+        jax.ShapeDtypeStruct((DATES, COL_DEV), BF16),
+        jax.ShapeDtypeStruct((2, 1, COL_DEV), F32),
+    )
+    operands = (
+        incidence.T,
+        coherent,
+        jnp.asarray(angle_tables()),
+        jnp.asarray(smoothing_matrix()),
+        jnp.asarray(column_scales()),
+        phases.reshape(ifgs, COL_DEV),
+    )
     corrected, trend_fit = pl.pallas_call(
         screen_kernel,
-        out_shape=(
-            jax.ShapeDtypeStruct((DATES, COL_DEV), BF16),
-            jax.ShapeDtypeStruct((2, 1, COL_DEV), F32),
-        ),
-        in_specs=[anywhere] * 6,
-        out_specs=(anywhere, anywhere),
+        out_shape=results,
+        in_specs=[in_hbm] * 6,
+        out_specs=(in_vmem, in_vmem),
         scratch_shapes=[
             pltpu.VMEM((2, ifgs), jnp.int32),
             pltpu.VMEM((1, COL_DEV), jnp.int32),
@@ -409,12 +447,12 @@
             pltpu.VMEM((256, 256), F32),
             pltpu.VMEM((2, 1, 128), F32),
             pltpu.VMEM((ifgs, COL_DEV), BF16),
-            pltpu.VMEM((DATES, COL_DEV), BF16),
-            pltpu.VMEM((2, 1, COL_DEV), F32),
             pltpu.VMEM((2 * FREQS, COL_DEV), BF16),
             pltpu.VMEM((DATES, COL_DEV), F32),
+            pltpu.VMEM((DATES, COL_DEV), BF16),
             pltpu.VMEM((DATES, ifgs), BF16),
-            pltpu.VMEM((DATES, 2 * FREQS), F32),
+            pltpu.VMEM((PLANE, 32, 128), BF16),
+            pltpu.VMEM((PLANE, 32, 128), BF16),
             pltpu.VMEM((PLANE, 32, 128), BF16),
             pltpu.VMEM((PLANE, 32, 128), BF16),
             pltpu.VMEM((DEPTH, 16, 128), BF16),
@@ -423,24 +461,26 @@
             pltpu.VMEM((DEPTH, 16, 128), BF16),
             pltpu.VMEM((SHELF, 32, 128), BF16),
             pltpu.VMEM((PLANE, 32, 128), BF16),
-            pltpu.VMEM((DATES, 2 * FREQS), BF16),
+            pltpu.VMEM((PLANE, 32, 128), BF16),
+            pltpu.VMEM((HALF, 2 * FREQS), BF16),
             pltpu.SemaphoreType.DMA((6,)),
-            pltpu.SemaphoreType.DMA((COL_DEV // TILE + 1,)),
-            pltpu.SemaphoreType.DMA((4,)),
-            pltpu.SemaphoreType.DMA((4,)),
+            pltpu.SemaphoreType.DMA((6,)),
+            pltpu.SemaphoreType.DMA((6,)),
         ],
         compiler_params=pltpu.CompilerParams(
-            collective_id=0, has_side_effects=True, vmem_limit_bytes=64 * 2**20
+            collective_id=0, has_side_effects=True, vmem_limit_bytes=36 * 2**20
         ),
         name="screen",
-    )(
-        incidence.T,
-        coherent,
-        jnp.asarray(angle_tables()),
-        jnp.asarray(smoothing_matrix()),
-        jnp.asarray(column_scales()),
-        phases.reshape(ifgs, COL_DEV),
-    )
+    )(*(pltpu.with_memory_space_constraint(operand, pltpu.HBM) for operand in operands))
+    corrected, trend_fit = pl.pallas_call(
+        store_kernel,
+        out_shape=results,
+        in_specs=[in_vmem] * 2,
+        out_specs=(in_hbm, in_hbm),
+        scratch_shapes=[pltpu.SemaphoreType.DMA((2,))],
+        compiler_params=pltpu.CompilerParams(vmem_limit_bytes=8 * 2**20),
+        name="store",
+    )(corrected, trend_fit)
     return (corrected.reshape(DATES, 1, COL_DEV), trend_fit)
 
 

time: 54.1 us -> 49.4 us (0.913)
  local copies, waits for them, and re-layouts: 3.63 us -> 0 us
  Pallas kernels: 49.6 us -> 48.7 us
    unnamed x2 -> x0, local copies, waits for them, and re-layouts: 3.63 us -> none
    pallas_call x1 -> x2, Pallas kernels: 49.6 us -> 48.7 us  [the longest x1 47.7 us: per_device(): pl.pallas_call(screen_kernel, out_shape=results, in_specs=[in_hbm] * 6, o...]
where the time goes in v2:
time: 49.4 us; the launch traced here: 49.3 us
  Pallas kernels  48.7 us (99%)
  between operations  0.64 us (1%)
    pallas_call x1, Pallas kernels, per_device(): pl.pallas_call(screen_kernel, out_shape=results, in_specs=[in_hbm] * 6, o...  47.7 us
    pallas_call x1, Pallas kernels, per_device(): pl.pallas_call(store_kernel, out_shape=results, in_specs=[in_vmem] * 2, o...  0.99 us

profile of v2, /device:TPU:1, one launch (start us, length us, event | category | flops | bytes accessed | tf_op | source)
XLA Modules:
  0.0 49.3 jit_solution(15183267630161109298)
XLA Ops:
  0.6 47.7 %screen.1 = (bf16[256,2048]{1,0:T(8,128)(2,1)S(1)}, f32[2,1,2048]{2,1,0:T(1,128)S(1)}) custom-call(s32[2,600]{1,0:T(2,128)} %bitcast.4, s32[1,2048]{1,0:T(1,128)} %coherent_hbm.1, f32[4,256,128]{2,1,0:T(8,128)} %constant.6.clone.angles_hbm, f32[256,256]{1,0:T(8,128)} %constant.7.clone.smooth_hbm, f32[2,1,128]{2,1,0:T(1,128)} %constant.8.clone.scale_hbm, ...), custom_call_target="tpu_custom_call" | custom-call | tf_op jit(solution)/shard_map/screen/pallas_call | solution.py:438
  48.3 1.0 %store.1 = (bf16[256,2048]{1,0:T(8,128)(2,1)}, f32[2,1,2048]{2,1,0:T(1,128)}) custom-call(bf16[256,2048]{1,0:T(8,128)(2,1)S(1)} %get-tuple-element.6.corrected_ref, f32[2,1,2048]{2,1,0:T(1,128)S(1)} %get-tuple-element.7.trend_ref), custom_call_target="tpu_custom_call" | custom-call | tf_op jit(solution)/shard_map/store/pallas_call | solution.py:475

commit v3 on v2

--- a/solution.py
+++ b/solution.py
@@ -1,3 +1,4 @@
+import functools
 import math
 
 import jax
@@ -80,10 +81,10 @@
 
 
 def block_product(a, b):
-    total = a[:, 0:1, :] * b[0][None]
-    for k in range(1, 8):
-        total = total + a[:, k : k + 1, :] * b[k][None]
-    return total
+    terms = [a[:, k : k + 1, :] * b[k][None] for k in range(8)]
+    while len(terms) > 1:
+        terms = [one + two for one, two in zip(terms[::2], terms[1::2])]
+    return terms[0]
 
 
 def reciprocal(x):
@@ -95,14 +96,21 @@
 def block_inverse(d):
     sub = iota((8, 128), 0)
     rows = [d[i] for i in range(8)]
-    for k in range(8):
-        pivot = reciprocal(rows[k][k : k + 1, :])
-        pivot_row = jnp.where(sub == k, pivot, rows[k] * pivot)
+    for k in range(0, 8, 2):
+        a, b = rows[k][k : k + 1, :], rows[k][k + 1 : k + 2, :]
+        c, e = rows[k + 1][k : k + 1, :], rows[k + 1][k + 1 : k + 2, :]
+        scale = reciprocal(a * e - b * c)
+        one, two = sub == k, sub == k + 1
+        first = jnp.where(one, 1.0, jnp.where(two, 0.0, rows[k]))
+        second = jnp.where(one, 0.0, jnp.where(two, 1.0, rows[k + 1]))
+        top = (e * scale) * first - (b * scale) * second
+        bottom = (a * scale) * second - (c * scale) * first
         for i in range(8):
-            if i != k:
-                factor = rows[i][k : k + 1, :]
-                rows[i] = jnp.where(sub == k, 0.0, rows[i]) - factor * pivot_row
-        rows[k] = pivot_row
+            if i not in (k, k + 1):
+                f, g = rows[i][k : k + 1, :], rows[i][k + 1 : k + 2, :]
+                rest = jnp.where(one | two, 0.0, rows[i])
+                rows[i] = rest - (f * top + g * bottom)
+        rows[k], rows[k + 1] = top, bottom
     return jnp.stack(rows)
 
 
@@ -121,7 +129,7 @@
     )
 
 
-def pseudo_inverse(incidence):
+def pseudo_inverse(incidence, beside):
     count = incidence.shape[1]
     primary, secondary = incidence[0:1, :], incidence[1:2, :]
     dates = iota((DATES, count), 0)
@@ -163,6 +171,7 @@
     total = None
     step = 1
     while step < BLOCKS:
+        beside()
         inverse = block_inverse(diag)
         near = jnp.where(first, lane_roll(inverse, step), lane_roll(inverse, 128 - step))
         gain = block_product(jnp.where(first, below, above), near)
@@ -186,27 +195,27 @@
             below = jnp.where(first, links, swapped)
             above = jnp.where(first, swapped, links)
         step *= 2
+    design_t = design_t.astype(BF16)
+    reduced = dot(
+        jnp.concatenate(split(total)[::-1], axis=1),
+        jnp.concatenate([design_t, design_t, design_t], axis=0),
+    )
     final = jnp.where(col_block == row_block, blocks_of(block_inverse(diag), 1), 0.0)
-    inverse = dot_split(split(final), split(total))
-    design_t = design_t.astype(BF16)
-    return dot(
-        jnp.concatenate(split(inverse)[::-1], axis=1),
-        jnp.concatenate([design_t, design_t, design_t], axis=0),
-    ).astype(BF16)
+    return dot_split(split(final), split(reduced)).astype(BF16)
 
 
 def part_index():
     return lax.axis_index("section") * 2 + lax.axis_index("sub")
 
 
-def fill_table(angles_ref, table_ref):
-    @pl.loop(0, FREQS // 64)
-    def _(group):
-        first = pl.multiple_of(group * 64, 64)
-        rows, sin_rows = pl.ds(first, 64), pl.ds(first + FREQS, 64)
+def table_filler(angles_ref, table_ref):
+    part = part_index()
+
+    def fill(first):
+        rows, sin_rows = slice(first, first + 64), slice(FREQS + first, FREQS + first + 64)
         cos, sin = angles_ref[0, rows, :], angles_ref[1, rows, :]
         step_cos, step_sin = angles_ref[2, rows, :], angles_ref[3, rows, :]
-        quarter = ((iota((64, 128), 0) + first) * part_index()) & 3
+        quarter = ((iota((64, 128), 0) + first) * part) & 3
         odd, minus = (quarter & 1) == 1, quarter >= 2
         cos, sin = jnp.where(odd, -sin, cos), jnp.where(odd, cos, sin)
         cos, sin = jnp.where(minus, -cos, cos), jnp.where(minus, -sin, sin)
@@ -215,6 +224,9 @@
             table_ref[rows, cols] = cos.astype(BF16)
             table_ref[sin_rows, cols] = (-sin).astype(BF16)
             cos, sin = cos * step_cos - sin * step_sin, sin * step_cos + cos * step_sin
+
+    steps = [functools.partial(fill, first) for first in range(0, FREQS, 64)]
+    return lambda: steps.pop()() if steps else None
 
 
 def regroup_matrix(inverse):
@@ -294,10 +306,9 @@
     for device in [partner] + [device for _, _, device in plane + column]:
         pl.semaphore_signal(barrier, inc=1, device_id=device, device_id_type=MESH)
 
+    loads[0].wait()
     loads[1].wait()
-    fill_table(angles_ref, table_ref)
-    loads[0].wait()
-    map_ref[...] = pseudo_inverse(incidence_ref[...])
+    map_ref[...] = pseudo_inverse(incidence_ref[...], table_filler(angles_ref, table_ref))
     epochs = (2.0 * iota((DATES, 1), 0).astype(F32) - (DATES - 1)) / (DATES - 1)
     spread = sum(((2.0 * n - (DATES - 1)) / (DATES - 1)) ** 2 for n in range(DATES))
     for load in loads[2:]:

time: 49.4 us -> 49.3 us (level)
  no operation moved by 1% of the time
where the time goes in v3:
time: 49.3 us; the launch traced here: 49.1 us
  Pallas kernels  48.5 us (98%)
  between operations  0.64 us (1%)
    pallas_call x1, Pallas kernels, per_device(): pl.pallas_call(screen_kernel, out_shape=results, in_specs=[in_hbm] * 6, o...  47.5 us
    pallas_call x1, Pallas kernels, per_device(): pl.pallas_call(store_kernel, out_shape=results, in_specs=[in_vmem] * 2, o...  0.99 us

profile of v3, /device:TPU:1, one launch (start us, length us, event | category | flops | bytes accessed | tf_op | source)
XLA Modules:
  0.0 49.1 jit_solution(15779345919323951526)
XLA Ops:
  0.6 47.5 %screen.1 = (bf16[256,2048]{1,0:T(8,128)(2,1)S(1)}, f32[2,1,2048]{2,1,0:T(1,128)S(1)}) custom-call(s32[2,600]{1,0:T(2,128)} %bitcast.4, s32[1,2048]{1,0:T(1,128)} %coherent_hbm.1, f32[4,256,128]{2,1,0:T(8,128)} %constant.6.clone.angles_hbm, f32[256,256]{1,0:T(8,128)} %constant.7.clone.smooth_hbm, f32[2,1,128]{2,1,0:T(1,128)} %constant.8.clone.scale_hbm, ...), custom_call_target="tpu_custom_call" | custom-call | tf_op jit(solution)/shard_map/screen/pallas_call | solution.py:449
  48.1 1.0 %store.1 = (bf16[256,2048]{1,0:T(8,128)(2,1)}, f32[2,1,2048]{2,1,0:T(1,128)}) custom-call(bf16[256,2048]{1,0:T(8,128)(2,1)S(1)} %get-tuple-element.6.corrected_ref, f32[2,1,2048]{2,1,0:T(1,128)S(1)} %get-tuple-element.7.trend_ref), custom_call_target="tpu_custom_call" | custom-call | tf_op jit(solution)/shard_map/store/pallas_call | solution.py:486

commit v4 on v3

--- a/solution.py
+++ b/solution.py
@@ -229,11 +229,9 @@
     return lambda: steps.pop()() if steps else None
 
 
-def regroup_matrix(inverse):
-    out, source = iota((256, 256), 0), iota((256, 256), 1)
-    if inverse:
-        out, source = source, out
-    return hot(source == ((out >> 1) & 7) * 32 + (out >> 4) * 2 + (out & 1)).astype(BF16)
+def regroup_matrix():
+    out, source = iota((128, 128), 0), iota((128, 128), 1)
+    return hot(source == ((out >> 1) & 7) * 16 + (out >> 4) * 2 + (out & 1)).astype(BF16)
 
 
 def screen_kernel(
@@ -292,18 +290,28 @@
     me = sub * 8 + y * 4 + x
     subs, ys = (sub, 1 - sub), (y, 1 - y)
     xs = [(x + hop) % 4 for hop in (2, 1, 3, 0)]
-    zs = [(z + hop) % 16 for hop in (8, 7, 9, 6, 10, 5, 11, 4, 12, 3, 13, 2, 14, 1, 15)]
     plane = [
         (b * 8 + c * 4 + d, c * 4 + d, (section, c * 64 + z * 4 + d, b))
         for d in xs
         for b in subs[::-1]
         for c in ys[::-1]
     ][:-1]
-    column = [(other, other, (section, y * 64 + other * 4 + x, sub)) for other in zs]
+    own, away = z % 2, 1 - z % 2
+    pairs = [(z // 2 + hop) % 8 for hop in (4, 3, 5, 2, 6, 1, 7, 0)]
+
+    def column(pair, parity):
+        other = pair * 2 + parity
+        return other, (section, y * 64 + other * 4 + x, sub)
+
+    lines = [
+        [(pair, *column(pair, away)) for pair in pairs],
+        [(pair, *column(pair, own)) for pair in pairs[:-1]],
+    ]
     partner = (1 - section, grp, sub)
 
     barrier = pltpu.get_barrier_semaphore()
-    for device in [partner] + [device for _, _, device in plane + column]:
+    peers = [partner] + [device for _, _, device in plane + lines[0] + lines[1]]
+    for device in peers:
         pl.semaphore_signal(barrier, inc=1, device_id=device, device_id_type=MESH)
 
     loads[0].wait()
@@ -332,75 +340,85 @@
         row, col = number // 4 * 32, number % 4 * 128
         return array[row : row + 32, col : col + 128]
 
-    pl.semaphore_wait(barrier, 1 + len(plane) + len(column))
+    pl.semaphore_wait(barrier, len(peers))
 
     theirs = dot_nt(residual_ref[half_rows(1 - section), :], table_ref[...]).astype(BF16)
     for number in range(PLANE):
         pair_out[number] = block(theirs, number)
-    give = pltpu.make_async_remote_copy(
-        src_ref=pair_out,
-        dst_ref=pair_in,
-        send_sem=send_sems.at[4],
-        recv_sem=recv_sems.at[4],
-        device_id=partner,
-        device_id_type=MESH,
-    )
+    def copy(number, source, target, device):
+        return pltpu.make_async_remote_copy(
+            src_ref=source,
+            dst_ref=target,
+            send_sem=send_sems.at[number],
+            recv_sem=recv_sems.at[number],
+            device_id=device,
+            device_id_type=MESH,
+        )
+
+    def wait(sems, number, blocks):
+        pltpu.make_async_copy(blocks, blocks, sems.at[number]).wait()
+
+    some = [up_in.at[pl.ds(0, len(line))] for line in lines]
+    most = back_in.at[0, pl.ds(0, len(plane))]
+
+    give = copy(10, pair_out, pair_in, partner)
     give.start()
     ours = dot_nt(residual_ref[half_rows(section), :], table_ref[...])
     give.wait_recv()
     for number in range(PLANE):
-        part_out[number] = (block(ours, number) + pair_in[number].astype(F32)).astype(BF16)
-
-    def exchange(phase, mine, partners, source, target):
-        for other, row, device in partners:
-            pltpu.make_async_remote_copy(
-                src_ref=source(other, row),
-                dst_ref=target.at[mine],
-                send_sem=send_sems.at[phase],
-                recv_sem=recv_sems.at[phase],
-                device_id=device,
-                device_id_type=MESH,
-            ).start()
-        target[mine] = source(mine, lax.rem(mine, SHELF))[...]
-
-    def arrived(phase, target, sems):
-        blocks = target.at[pl.ds(0, target.shape[0] - 1)]
-        pltpu.make_async_copy(blocks, blocks, sems.at[phase]).wait()
-
-    exchange(0, me, plane, lambda other, row: part_out.at[other], part_in)
+        both = (block(ours, number) + pair_in[number].astype(F32)).astype(BF16)
+        part_out[0, number] = both[:16]
+        part_out[1, number] = both[16:]
+
+    for turn, parity in enumerate((away, own)):
+        for other, _, device in plane:
+            copy(turn, part_out.at[parity, other], part_in.at[parity, me], device).start()
+        part_in[parity, me] = part_out[parity, me]
+
     smooth = smooth_ref[...]
     smooth_high = smooth.astype(BF16)
     smooth_low = (smooth - smooth_high.astype(F32)).astype(BF16)
-    regroup, ungroup = regroup_matrix(False), regroup_matrix(True)
-    arrived(0, part_in, recv_sems)
-    row_sum = jnp.sum(part_in[...].astype(F32).reshape(2, 256, 128), axis=0).astype(BF16)
-    up_out[...] = dot(regroup, row_sum).astype(BF16).reshape(DEPTH, 16, 128)
-    exchange(1, z, column, lambda other, row: up_out.at[other], up_in)
-    arrived(1, up_in, recv_sems)
+    regroup = regroup_matrix()
+
+    for turn, parity in enumerate((away, own)):
+        wait(recv_sems, turn, most)
+        row_sum = jnp.sum(part_in[parity].astype(F32).reshape(2, 128, 128), axis=0).astype(BF16)
+        up_out[parity] = dot(regroup, row_sum).astype(BF16).reshape(8, 16, 128)
+        for pair, _, device in lines[turn]:
+            copy(2 + turn, up_out.at[parity, pair], up_in.at[z], device).start()
+    up_in[z] = up_out[own, z // 2]
+
+    wait(recv_sems, 2, some[0])
+    wait(recv_sems, 3, some[1])
     rows = up_in[...].reshape(256, 128)
     smoothed = dot(smooth_high, rows) + dot(smooth_low, rows)
     down_out[...] = (smoothed * scale_ref[me % 2]).astype(BF16).reshape(DEPTH, 16, 128)
-    exchange(2, z, column, lambda other, row: down_out.at[other], down_in)
-    arrived(2, down_in, recv_sems)
-    whole = down_in[...].reshape(256, 128)
-    back_out[...] = dot(ungroup, whole).astype(BF16).reshape(SHELF, 32, 128)
-    exchange(3, me, plane, lambda other, row: back_out.at[row], back_in)
-    arrived(3, back_in, recv_sems)
-
-    swap = pltpu.make_async_remote_copy(
-        src_ref=back_in,
-        dst_ref=swap_in,
-        send_sem=send_sems.at[5],
-        recv_sem=recv_sems.at[5],
-        device_id=partner,
-        device_id_type=MESH,
-    )
-    swap.start()
+    for turn in range(2):
+        for _, other, device in lines[turn]:
+            copy(4 + turn, down_out.at[other], down_in.at[own, z // 2], device).start()
+    down_in[own, z // 2] = down_out[z]
+
+    for turn, parity in enumerate((away, own)):
+        wait(recv_sems, 4 + turn, some[turn])
+        whole = down_in[parity].reshape(128, 128)
+        back_out[parity] = dot(regroup, whole).astype(BF16).reshape(SHELF, 16, 128)
+        for _, row, device in plane:
+            copy(6 + turn, back_out.at[parity, row], back_in.at[parity, me], device).start()
+        back_in[parity, me] = back_out[parity, lax.rem(me, SHELF)]
+
+    swaps = [
+        copy(8 + turn, back_in.at[parity], swap_in.at[parity], partner)
+        for turn, parity in enumerate((away, own))
+    ]
+    for turn, swap in enumerate(swaps):
+        wait(recv_sems, 6 + turn, most)
+        swap.start()
 
     def correct(half, weights):
         for number in range(PLANE):
             row, col = number // 4 * 32, number % 4 * 128
-            flat_ref[row : row + 32, col : col + 128] = weights[number]
+            flat_ref[row : row + 16, col : col + 128] = weights[0, number]
+            flat_ref[row + 16 : row + 32, col : col + 128] = weights[1, number]
         dates = half_rows(half)
         for tile in range(COL_DEV // TILE):
             cols = slice(tile * TILE, tile * TILE + TILE)
@@ -410,13 +428,16 @@
 
     correct(section, back_in)
     give.wait_send()
-    arrived(0, part_in, send_sems)
-    arrived(1, up_in, send_sems)
-    arrived(2, down_in, send_sems)
-    arrived(3, back_in, send_sems)
-    swap.wait_recv()
+    for turn in range(2):
+        wait(send_sems, turn, most)
+        wait(send_sems, 2 + turn, some[turn])
+        wait(send_sems, 4 + turn, some[turn])
+        wait(send_sems, 6 + turn, most)
+    for swap in swaps:
+        swap.wait_recv()
     correct(1 - section, swap_in)
-    swap.wait_send()
+    for swap in swaps:
+        swap.wait_send()
 
 
 def store_kernel(corrected_ref, trend_ref, corrected_hbm, trend_hbm, sems):
@@ -464,19 +485,19 @@
             pltpu.VMEM((DATES, ifgs), BF16),
             pltpu.VMEM((PLANE, 32, 128), BF16),
             pltpu.VMEM((PLANE, 32, 128), BF16),
-            pltpu.VMEM((PLANE, 32, 128), BF16),
-            pltpu.VMEM((PLANE, 32, 128), BF16),
+            pltpu.VMEM((2, PLANE, 16, 128), BF16),
+            pltpu.VMEM((2, PLANE, 16, 128), BF16),
+            pltpu.VMEM((2, 8, 16, 128), BF16),
             pltpu.VMEM((DEPTH, 16, 128), BF16),
             pltpu.VMEM((DEPTH, 16, 128), BF16),
-            pltpu.VMEM((DEPTH, 16, 128), BF16),
-            pltpu.VMEM((DEPTH, 16, 128), BF16),
-            pltpu.VMEM((SHELF, 32, 128), BF16),
-            pltpu.VMEM((PLANE, 32, 128), BF16),
-            pltpu.VMEM((PLANE, 32, 128), BF16),
+            pltpu.VMEM((2, 8, 16, 128), BF16),
+            pltpu.VMEM((2, SHELF, 16, 128), BF16),
+            pltpu.VMEM((2, PLANE, 16, 128), BF16),
+            pltpu.VMEM((2, PLANE, 16, 128), BF16),
             pltpu.VMEM((HALF, 2 * FREQS), BF16),
             pltpu.SemaphoreType.DMA((6,)),
-            pltpu.SemaphoreType.DMA((6,)),
-            pltpu.SemaphoreType.DMA((6,)),
+            pltpu.SemaphoreType.DMA((11,)),
+            pltpu.SemaphoreType.DMA((11,)),
         ],
         compiler_params=pltpu.CompilerParams(
             collective_id=0, has_side_effects=True, vmem_limit_bytes=36 * 2**20

time: 49.3 us -> 49.7 us (level)
  no operation moved by 1% of the time
where the time goes in v4:
time: 49.7 us; the launch traced here: 49.6 us
  Pallas kernels  48.9 us (98%)
  between operations  0.64 us (1%)
    pallas_call x1, Pallas kernels, per_device(): pl.pallas_call(screen_kernel, out_shape=results, in_specs=[in_hbm] * 6, o...  48 us

profile of v4, /device:TPU:1, one launch (start us, length us, event | category | flops | bytes accessed | tf_op | source)
XLA Modules:
  0.0 49.6 jit_solution(807598855969680502)
XLA Ops:
  0.6 48.0 %screen.1 = (bf16[256,2048]{1,0:T(8,128)(2,1)S(1)}, f32[2,1,2048]{2,1,0:T(1,128)S(1)}) custom-call(s32[2,600]{1,0:T(2,128)} %bitcast.4, s32[1,2048]{1,0:T(1,128)} %coherent_hbm.1, f32[4,256,128]{2,1,0:T(8,128)} %constant.6.clone.angles_hbm, f32[256,256]{1,0:T(8,128)} %constant.7.clone.smooth_hbm, f32[2,1,128]{2,1,0:T(1,128)} %constant.8.clone.scale_hbm, ...), custom_call_target="tpu_custom_call" | custom-call | tf_op jit(solution)/shard_map/screen/pallas_call | solution.py:470
  48.6 1.0 %store.1 = (bf16[256,2048]{1,0:T(8,128)(2,1)}, f32[2,1,2048]{2,1,0:T(1,128)}) custom-call(bf16[256,2048]{1,0:T(8,128)(2,1)S(1)} %get-tuple-element.6.corrected_ref, f32[2,1,2048]{2,1,0:T(1,128)S(1)} %get-tuple-element.7.trend_ref), custom_call_target="tpu_custom_call" | custom-call | tf_op jit(solution)/shard_map/store/pallas_call | solution.py:507

commit v5 on v3

--- a/solution.py
+++ b/solution.py
@@ -1,4 +1,3 @@
-import functools
 import math
 
 import jax
@@ -129,7 +128,7 @@
     )
 
 
-def pseudo_inverse(incidence, beside):
+def pseudo_inverse(incidence, total_ref):
     count = incidence.shape[1]
     primary, secondary = incidence[0:1, :], incidence[1:2, :]
     dates = iota((DATES, count), 0)
@@ -168,33 +167,38 @@
         rows = jnp.where(own_row[:count], dot_nt(take[:count], terms), 0.0).astype(BF16)
         return dot(rows, spread)
 
-    total = None
-    step = 1
-    while step < BLOCKS:
-        beside()
+    def apply(gain, step):
+        sides = blocks_of(gain, 2)
+        gamma = jnp.where(
+            col_block == row_block - step,
+            sides[:DATES],
+            jnp.where(col_block == row_block + step, sides[DATES:], 0.0),
+        )
+        total = total_ref[...]
+        total_ref[...] = total - dot_split(split(gamma), split(total))
+
+    def level(_, carry):
+        step, last_step, diag, below, above, last_gain = carry
+        apply(last_gain, last_step)
         inverse = block_inverse(diag)
         near = jnp.where(first, lane_roll(inverse, step), lane_roll(inverse, 128 - step))
         gain = block_product(jnp.where(first, below, above), near)
         back = jnp.where(first, lane_roll(above, step), lane_roll(below, 128 - step))
         change = block_product(gain, back)
         diag = diag - change - lane_roll(change, BLOCKS)
-        sides = blocks_of(gain, 2)
-        gamma = jnp.where(
-            col_block == row_block - step,
-            sides[:DATES],
-            jnp.where(col_block == row_block + step, sides[DATES:], 0.0),
-        )
-        if total is None:
-            total = hot(iota((DATES, DATES), 0) == iota((DATES, DATES), 1)) - gamma
-        else:
-            total = total - dot_split(split(gamma), split(total))
-        if 2 * step < BLOCKS:
-            far = jnp.where(first, lane_roll(below, step), lane_roll(above, 128 - step))
-            links = -block_product(gain, far)
-            swapped = lane_roll(links, BLOCKS)
-            below = jnp.where(first, links, swapped)
-            above = jnp.where(first, swapped, links)
-        step *= 2
+        far = jnp.where(first, lane_roll(below, step), lane_roll(above, 128 - step))
+        links = -block_product(gain, far)
+        swapped = lane_roll(links, BLOCKS)
+        below = jnp.where(first, links, swapped)
+        above = jnp.where(first, swapped, links)
+        return step * 2, step, diag, below, above, gain
+
+    total_ref[...] = hot(iota((DATES, DATES), 0) == iota((DATES, DATES), 1))
+    start = (jnp.int32(1), jnp.int32(0), diag, below, above, jnp.zeros((8, 8, 128), F32))
+    levels = BLOCKS.bit_length() - 1
+    _, last_step, diag, _, _, last_gain = lax.fori_loop(0, levels, level, start)
+    apply(last_gain, last_step)
+    total = total_ref[...]
     design_t = design_t.astype(BF16)
     reduced = dot(
         jnp.concatenate(split(total)[::-1], axis=1),
@@ -208,14 +212,14 @@
     return lax.axis_index("section") * 2 + lax.axis_index("sub")
 
 
-def table_filler(angles_ref, table_ref):
-    part = part_index()
-
-    def fill(first):
-        rows, sin_rows = slice(first, first + 64), slice(FREQS + first, FREQS + first + 64)
+def fill_table(angles_ref, table_ref):
+    @pl.loop(0, FREQS // 64)
+    def _(group):
+        first = pl.multiple_of(group * 64, 64)
+        rows, sin_rows = pl.ds(first, 64), pl.ds(first + FREQS, 64)
         cos, sin = angles_ref[0, rows, :], angles_ref[1, rows, :]
         step_cos, step_sin = angles_ref[2, rows, :], angles_ref[3, rows, :]
-        quarter = ((iota((64, 128), 0) + first) * part) & 3
+        quarter = ((iota((64, 128), 0) + first) * part_index()) & 3
         odd, minus = (quarter & 1) == 1, quarter >= 2
         cos, sin = jnp.where(odd, -sin, cos), jnp.where(odd, cos, sin)
         cos, sin = jnp.where(minus, -cos, cos), jnp.where(minus, -sin, sin)
@@ -224,9 +228,6 @@
             table_ref[rows, cols] = cos.astype(BF16)
             table_ref[sin_rows, cols] = (-sin).astype(BF16)
             cos, sin = cos * step_cos - sin * step_sin, sin * step_cos + cos * step_sin
-
-    steps = [functools.partial(fill, first) for first in range(0, FREQS, 64)]
-    return lambda: steps.pop()() if steps else None
 
 
 def regroup_matrix(inverse):
@@ -253,8 +254,9 @@
     phases_ref,
     table_ref,
     series_ref,
-    residual_ref,
+    spectrum_ref,
     map_ref,
+    total_ref,
     pair_out,
     pair_in,
     part_out,
@@ -290,32 +292,40 @@
     section, grp, sub = (lax.axis_index(name) for name in ("section", "grp", "sub"))
     y, z, x = grp // 64, grp // 4 % 16, grp % 4
     me = sub * 8 + y * 4 + x
-    subs, ys = (sub, 1 - sub), (y, 1 - y)
-    xs = [(x + hop) % 4 for hop in (2, 1, 3, 0)]
-    zs = [(z + hop) % 16 for hop in (8, 7, 9, 6, 10, 5, 11, 4, 12, 3, 13, 2, 14, 1, 15)]
-    plane = [
-        (b * 8 + c * 4 + d, c * 4 + d, (section, c * 64 + z * 4 + d, b))
-        for d in xs
-        for b in subs[::-1]
-        for c in ys[::-1]
-    ][:-1]
-    column = [(other, other, (section, y * 64 + other * 4 + x, sub)) for other in zs]
+    def in_plane(hop):
+        other = lax.rem(me + hop, PLANE)
+        row = lax.rem(other, SHELF)
+        x_other = lax.rem(other, 4)
+        grp_other = lax.div(row, 4) * 64 + z * 4 + x_other
+        return other, row, (section, grp_other, lax.div(other, SHELF))
+
+    def along_z(hop):
+        other = lax.rem(z + hop, DEPTH)
+        return other, other, (section, grp + (other - z) * 4, sub)
+
     partner = (1 - section, grp, sub)
 
     barrier = pltpu.get_barrier_semaphore()
-    for device in [partner] + [device for _, _, device in plane + column]:
-        pl.semaphore_signal(barrier, inc=1, device_id=device, device_id_type=MESH)
-
+    pl.semaphore_signal(barrier, inc=1, device_id=partner, device_id_type=MESH)
+
+    @pl.loop(1, PLANE)
+    def _(hop):
+        for near in (in_plane, along_z):
+            pl.semaphore_signal(barrier, inc=1, device_id=near(hop)[2], device_id_type=MESH)
+
+    loads[1].wait()
+    fill_table(angles_ref, table_ref)
     loads[0].wait()
-    loads[1].wait()
-    map_ref[...] = pseudo_inverse(incidence_ref[...], table_filler(angles_ref, table_ref))
+    map_ref[...] = pseudo_inverse(incidence_ref[...], total_ref)
+    spectrum_ref[...] = jnp.zeros_like(spectrum_ref)
     epochs = (2.0 * iota((DATES, 1), 0).astype(F32) - (DATES - 1)) / (DATES - 1)
     spread = sum(((2.0 * n - (DATES - 1)) / (DATES - 1)) ** 2 for n in range(DATES))
     for load in loads[2:]:
         load.wait()
 
-    for tile in range(COL_DEV // TILE):
-        cols = slice(tile * TILE, tile * TILE + TILE)
+    @pl.loop(0, COL_DEV // TILE)
+    def _(tile):
+        cols = pl.ds(pl.multiple_of(tile * TILE, TILE), TILE)
         series = dot(map_ref[...], phases_ref[:, cols])
         series_ref[:, cols] = series
         offset = jnp.sum(series, axis=0, keepdims=True) / DATES
@@ -323,7 +333,8 @@
         trend_ref[0, :, cols] = offset
         trend_ref[1, :, cols] = rate
         live = coherent_ref[:, cols].astype(F32)
-        residual_ref[:, cols] = (live * (series - offset - epochs * rate)).astype(BF16)
+        residual = (live * (series - offset - epochs * rate)).astype(BF16)
+        spectrum_ref[...] += dot_nt(residual, table_ref[:, cols])
 
     def half_rows(half):
         return pl.ds(pl.multiple_of(half * HALF, HALF), HALF)
@@ -332,9 +343,9 @@
         row, col = number // 4 * 32, number % 4 * 128
         return array[row : row + 32, col : col + 128]
 
-    pl.semaphore_wait(barrier, 1 + len(plane) + len(column))
-
-    theirs = dot_nt(residual_ref[half_rows(1 - section), :], table_ref[...]).astype(BF16)
+    pl.semaphore_wait(barrier, 1 + PLANE - 1 + DEPTH - 1)
+
+    theirs = spectrum_ref[half_rows(1 - section), :].astype(BF16)
     for number in range(PLANE):
         pair_out[number] = block(theirs, number)
     give = pltpu.make_async_remote_copy(
@@ -346,13 +357,15 @@
         device_id_type=MESH,
     )
     give.start()
-    ours = dot_nt(residual_ref[half_rows(section), :], table_ref[...])
+    ours = spectrum_ref[half_rows(section), :]
     give.wait_recv()
     for number in range(PLANE):
         part_out[number] = (block(ours, number) + pair_in[number].astype(F32)).astype(BF16)
 
-    def exchange(phase, mine, partners, source, target):
-        for other, row, device in partners:
+    def exchange(phase, mine, near, source, target):
+        @pl.loop(1, PLANE)
+        def _(hop):
+            other, row, device = near(hop)
             pltpu.make_async_remote_copy(
                 src_ref=source(other, row),
                 dst_ref=target.at[mine],
@@ -361,13 +374,14 @@
                 device_id=device,
                 device_id_type=MESH,
             ).start()
+
         target[mine] = source(mine, lax.rem(mine, SHELF))[...]
 
     def arrived(phase, target, sems):
         blocks = target.at[pl.ds(0, target.shape[0] - 1)]
         pltpu.make_async_copy(blocks, blocks, sems.at[phase]).wait()
 
-    exchange(0, me, plane, lambda other, row: part_out.at[other], part_in)
+    exchange(0, me, in_plane, lambda other, row: part_out.at[other], part_in)
     smooth = smooth_ref[...]
     smooth_high = smooth.astype(BF16)
     smooth_low = (smooth - smooth_high.astype(F32)).astype(BF16)
@@ -375,16 +389,16 @@
     arrived(0, part_in, recv_sems)
     row_sum = jnp.sum(part_in[...].astype(F32).reshape(2, 256, 128), axis=0).astype(BF16)
     up_out[...] = dot(regroup, row_sum).astype(BF16).reshape(DEPTH, 16, 128)
-    exchange(1, z, column, lambda other, row: up_out.at[other], up_in)
+    exchange(1, z, along_z, lambda other, row: up_out.at[other], up_in)
     arrived(1, up_in, recv_sems)
     rows = up_in[...].reshape(256, 128)
     smoothed = dot(smooth_high, rows) + dot(smooth_low, rows)
     down_out[...] = (smoothed * scale_ref[me % 2]).astype(BF16).reshape(DEPTH, 16, 128)
-    exchange(2, z, column, lambda other, row: down_out.at[other], down_in)
+    exchange(2, z, along_z, lambda other, row: down_out.at[other], down_in)
     arrived(2, down_in, recv_sems)
     whole = down_in[...].reshape(256, 128)
     back_out[...] = dot(ungroup, whole).astype(BF16).reshape(SHELF, 32, 128)
-    exchange(3, me, plane, lambda other, row: back_out.at[row], back_in)
+    exchange(3, me, in_plane, lambda other, row: back_out.at[row], back_in)
     arrived(3, back_in, recv_sems)
 
     swap = pltpu.make_async_remote_copy(
@@ -402,8 +416,10 @@
             row, col = number // 4 * 32, number % 4 * 128
             flat_ref[row : row + 32, col : col + 128] = weights[number]
         dates = half_rows(half)
-        for tile in range(COL_DEV // TILE):
-            cols = slice(tile * TILE, tile * TILE + TILE)
+
+        @pl.loop(0, COL_DEV // TILE)
+        def _(tile):
+            cols = pl.ds(pl.multiple_of(tile * TILE, TILE), TILE)
             screen = dot(flat_ref[...], table_ref[:, cols]).astype(BF16).astype(F32)
             live = coherent_ref[:, cols].astype(F32)
             corrected_ref[dates, cols] = (live * (series_ref[dates, cols] - screen)).astype(BF16)
@@ -460,8 +476,9 @@
             pltpu.VMEM((ifgs, COL_DEV), BF16),
             pltpu.VMEM((2 * FREQS, COL_DEV), BF16),
             pltpu.VMEM((DATES, COL_DEV), F32),
-            pltpu.VMEM((DATES, COL_DEV), BF16),
+            pltpu.VMEM((DATES, 2 * FREQS), F32),
             pltpu.VMEM((DATES, ifgs), BF16),
+            pltpu.VMEM((DATES, DATES), F32),
             pltpu.VMEM((PLANE, 32, 128), BF16),
             pltpu.VMEM((PLANE, 32, 128), BF16),
             pltpu.VMEM((PLANE, 32, 128), BF16),

time: 49.3 us -> 54.1 us (1.097)
  Pallas kernels: 48.5 us -> 53.3 us
    pallas_call x1, Pallas kernels: 47.5 us -> 52.3 us  [per_device(): pl.pallas_call(screen_kernel, out_shape=results, in_specs=[in_hbm] * 6, o...]
where the time goes in v5:
time: 54.1 us; the launch traced here: 53.9 us
  Pallas kernels  53.3 us (99%)
  between operations  0.64 us (1%)
    pallas_call x1, Pallas kernels, per_device(): pl.pallas_call(screen_kernel, out_shape=results, in_specs=[in_hbm] * 6, o...  52.3 us

profile of v5, /device:TPU:1, one launch (start us, length us, event | category | flops | bytes accessed | tf_op | source)
XLA Modules:
  0.0 53.9 jit_solution(16487368674261689559)
XLA Ops:
  0.6 52.3 %screen.1 = (bf16[256,2048]{1,0:T(8,128)(2,1)S(1)}, f32[2,1,2048]{2,1,0:T(1,128)S(1)}) custom-call(s32[2,600]{1,0:T(2,128)} %bitcast.4, s32[1,2048]{1,0:T(1,128)} %coherent_hbm.1, f32[4,256,128]{2,1,0:T(8,128)} %constant.6.clone.angles_hbm, f32[256,256]{1,0:T(8,128)} %constant.7.clone.smooth_hbm, f32[2,1,128]{2,1,0:T(1,128)} %constant.8.clone.scale_hbm, ...), custom_call_target="tpu_custom_call" | custom-call | tf_op jit(solution)/shard_map/screen/pallas_call | solution.py:465
  52.9 1.0 %store.1 = (bf16[256,2048]{1,0:T(8,128)(2,1)}, f32[2,1,2048]{2,1,0:T(1,128)}) custom-call(bf16[256,2048]{1,0:T(8,128)(2,1)S(1)} %get-tuple-element.6.corrected_ref, f32[2,1,2048]{2,1,0:T(1,128)S(1)} %get-tuple-element.7.trend_ref), custom_call_target="tpu_custom_call" | custom-call | tf_op jit(solution)/shard_map/store/pallas_call | solution.py:503

commit v6 on v3

--- a/solution.py
+++ b/solution.py
@@ -116,17 +116,12 @@
 
 def split(x):
     high = x.astype(BF16)
-    rest = x - high.astype(F32)
-    middle = rest.astype(BF16)
-    return high, middle, (rest - middle.astype(F32)).astype(BF16)
+    return high, (x - high.astype(F32)).astype(BF16)
 
 
 def dot_split(a, b):
-    (ah, am, al), (bh, bm, bl) = a, b
-    return dot(
-        jnp.concatenate([al, am, ah, am, ah, ah], axis=1),
-        jnp.concatenate([bh, bm, bl, bh, bm, bh], axis=0),
-    )
+    (ah, al), (bh, bl) = a, b
+    return dot(jnp.concatenate([al, ah, ah], axis=1), jnp.concatenate([bh, bl, bh], axis=0))
 
 
 def pseudo_inverse(incidence, beside):
@@ -157,8 +152,8 @@
 
     date = iota((2 * DATES, 128), 0)
     take = hot((date >> 3) == iota((2 * DATES, 128), 1)).astype(BF16)
-    own_row = ((iota((2 * DATES, 192), 1) >> 3) & 7) == (iota((2 * DATES, 192), 0) & 7)
-    spread = hot((iota((192, DATES), 1) & 7) == (iota((192, DATES), 0) & 7)).astype(BF16)
+    own_row = ((iota((2 * DATES, 128), 1) >> 3) & 7) == (iota((2 * DATES, 128), 0) & 7)
+    spread = hot((iota((128, DATES), 1) & 7) == (iota((128, DATES), 0) & 7)).astype(BF16)
     row_block = iota((DATES, DATES), 0) >> 3
     col_block = iota((DATES, DATES), 1) >> 3
 
@@ -198,7 +193,7 @@
     design_t = design_t.astype(BF16)
     reduced = dot(
         jnp.concatenate(split(total)[::-1], axis=1),
-        jnp.concatenate([design_t, design_t, design_t], axis=0),
+        jnp.concatenate([design_t, design_t], axis=0),
     )
     final = jnp.where(col_block == row_block, blocks_of(block_inverse(diag), 1), 0.0)
     return dot_split(split(final), split(reduced)).astype(BF16)
@@ -216,14 +211,17 @@
         cos, sin = angles_ref[0, rows, :], angles_ref[1, rows, :]
         step_cos, step_sin = angles_ref[2, rows, :], angles_ref[3, rows, :]
         quarter = ((iota((64, 128), 0) + first) * part) & 3
-        odd, minus = (quarter & 1) == 1, quarter >= 2
+        odd, flip = (quarter & 1) == 1, quarter >= 2
         cos, sin = jnp.where(odd, -sin, cos), jnp.where(odd, cos, sin)
-        cos, sin = jnp.where(minus, -cos, cos), jnp.where(minus, -sin, sin)
+        cos, sin = jnp.where(flip, -cos, cos), jnp.where(flip, -sin, sin)
+        cos_last, minus_last = cos * step_cos + sin * step_sin, cos * step_sin - sin * step_cos
+        minus, twice = -sin, 2.0 * step_cos
         for tile in range(COL_DEV // 128):
             cols = slice(tile * 128, tile * 128 + 128)
             table_ref[rows, cols] = cos.astype(BF16)
-            table_ref[sin_rows, cols] = (-sin).astype(BF16)
-            cos, sin = cos * step_cos - sin * step_sin, sin * step_cos + cos * step_sin
+            table_ref[sin_rows, cols] = minus.astype(BF16)
+            cos, cos_last = twice * cos - cos_last, cos
+            minus, minus_last = twice * minus - minus_last, minus
 
     steps = [functools.partial(fill, first) for first in range(0, FREQS, 64)]
     return lambda: steps.pop()() if steps else None

time: 49.3 us -> 47.8 us (0.970)
  Pallas kernels: 48.5 us -> 47 us
    pallas_call x1, Pallas kernels: 47.5 us -> 46 us  [per_device(): pl.pallas_call(screen_kernel, out_shape=results, in_specs=[in_hbm] * 6, o...]
where the time goes in v6:
time: 47.8 us; the launch traced here: 47.7 us
  Pallas kernels  47 us (98%)
  between operations  0.64 us (1%)
    pallas_call x1, Pallas kernels, per_device(): pl.pallas_call(screen_kernel, out_shape=results, in_specs=[in_hbm] * 6, o...  46 us
    pallas_call x1, Pallas kernels, per_device(): pl.pallas_call(store_kernel, out_shape=results, in_specs=[in_vmem] * 2, o...  0.99 us

profile of v6, /device:TPU:1, one launch (start us, length us, event | category | flops | bytes accessed | tf_op | source)
XLA Modules:
  0.0 47.7 jit_solution(1768631440636720165)
XLA Ops:
  0.6 46.0 %screen.1 = (bf16[256,2048]{1,0:T(8,128)(2,1)S(1)}, f32[2,1,2048]{2,1,0:T(1,128)S(1)}) custom-call(s32[2,600]{1,0:T(2,128)} %bitcast.4, s32[1,2048]{1,0:T(1,128)} %coherent_hbm.1, f32[4,256,128]{2,1,0:T(8,128)} %constant.6.clone.angles_hbm, f32[256,256]{1,0:T(8,128)} %constant.7.clone.smooth_hbm, f32[2,1,128]{2,1,0:T(1,128)} %constant.8.clone.scale_hbm, ...), custom_call_target="tpu_custom_call" | custom-call | tf_op jit(solution)/shard_map/screen/pallas_call | solution.py:447
  46.7 1.0 %store.1 = (bf16[256,2048]{1,0:T(8,128)(2,1)}, f32[2,1,2048]{2,1,0:T(1,128)}) custom-call(bf16[256,2048]{1,0:T(8,128)(2,1)S(1)} %get-tuple-element.6.corrected_ref, f32[2,1,2048]{2,1,0:T(1,128)S(1)} %get-tuple-element.7.trend_ref), custom_call_target="tpu_custom_call" | custom-call | tf_op jit(solution)/shard_map/store/pallas_call | solution.py:484

commit v7 on v6

--- a/solution.py
+++ b/solution.py
@@ -1,4 +1,3 @@
-import functools
 import math
 
 import jax
@@ -46,17 +45,16 @@
 
 
 def smoothing_matrix():
-    index = np.arange(DEPTH * SHELF * 2)
-    z, shelf, half = index // 16, index // 2 % 8, index % 2
+    index = np.arange(DEPTH * SHELF)
+    z, shelf = index // 8, index % 8
     row = shelf // 4 * 64 + z * 4 + shelf % 4
-    full = row_filter()[row[:, None], row[None, :]] * (half[:, None] == half[None, :])
-    return full.astype(np.float32)
+    return row_filter()[row[:, None], row[None, :]].astype(np.float32)
 
 
 def column_scales():
     frequency = np.arange(FREQS)
     scale = np.where(frequency == 0, 1.0, 2.0) * np.exp(-np.square(frequency / FREQS)) / COLS
-    return scale.astype(np.float32).reshape(2, 1, 128)
+    return np.repeat(scale.astype(np.float32)[:, None, None], 128, axis=2)
 
 
 def iota(shape, axis):
@@ -124,11 +122,27 @@
     return dot(jnp.concatenate([al, ah, ah], axis=1), jnp.concatenate([bh, bl, bh], axis=0))
 
 
-def pseudo_inverse(incidence, beside):
+def split_fully(x):
+    high, _ = split(x)
+    return (high, *split(x - high.astype(F32)))
+
+
+def dot_nt_fully(a, b):
+    (ah, am, al), (bh, bm, bl) = split_fully(a), split_fully(b)
+    return dot_nt(
+        jnp.concatenate([al, am, ah, am, ah, ah], axis=1),
+        jnp.concatenate([bh, bm, bl, bh, bm, bh], axis=1),
+    )
+
+
+def design_rows(incidence):
+    dates = iota((DATES, incidence.shape[1]), 0)
+    return (hot(dates == incidence[1:2, :]) - hot(dates == incidence[0:1, :])).astype(BF16)
+
+
+def pseudo_inverse(incidence, design_t):
     count = incidence.shape[1]
     primary, secondary = incidence[0:1, :], incidence[1:2, :]
-    dates = iota((DATES, count), 0)
-    design_t = hot(dates == secondary) - hot(dates == primary)
     p_in, p_block, s_in, s_block = primary & 7, primary >> 3, secondary & 7, secondary >> 3
     block = iota((128, count), 0) & (BLOCKS - 1)
     at_primary = hot(block == p_block).astype(BF16)
@@ -166,7 +180,6 @@
     total = None
     step = 1
     while step < BLOCKS:
-        beside()
         inverse = block_inverse(diag)
         near = jnp.where(first, lane_roll(inverse, step), lane_roll(inverse, 128 - step))
         gain = block_product(jnp.where(first, below, above), near)
@@ -190,20 +203,20 @@
             below = jnp.where(first, links, swapped)
             above = jnp.where(first, swapped, links)
         step *= 2
-    design_t = design_t.astype(BF16)
+        yield
     reduced = dot(
         jnp.concatenate(split(total)[::-1], axis=1),
         jnp.concatenate([design_t, design_t], axis=0),
     )
     final = jnp.where(col_block == row_block, blocks_of(block_inverse(diag), 1), 0.0)
-    return dot_split(split(final), split(reduced)).astype(BF16)
+    yield dot_split(split(final), split(reduced)).astype(BF16), total, final
 
 
 def part_index():
     return lax.axis_index("section") * 2 + lax.axis_index("sub")
 
 
-def table_filler(angles_ref, table_ref):
+def fill_table(angles_ref, table_ref):
     part = part_index()
 
     def fill(first):
@@ -223,15 +236,18 @@
             cos, cos_last = twice * cos - cos_last, cos
             minus, minus_last = twice * minus - minus_last, minus
 
-    steps = [functools.partial(fill, first) for first in range(0, FREQS, 64)]
-    return lambda: steps.pop()() if steps else None
-
-
-def regroup_matrix(inverse):
+    for first in range(0, FREQS, 64):
+        fill(first)
+
+
+def regroup_matrix():
+    out, source = iota((128, 128), 0), iota((128, 128), 1)
+    return hot(source == (out & 7) * 16 + (out >> 3)).astype(BF16)
+
+
+def ungroup_matrix():
     out, source = iota((256, 256), 0), iota((256, 256), 1)
-    if inverse:
-        out, source = source, out
-    return hot(source == ((out >> 1) & 7) * 32 + (out >> 4) * 2 + (out & 1)).astype(BF16)
+    return hot(source == (out & 15) * 16 + ((out >> 4) & 1) * 8 + (out >> 5)).astype(BF16)
 
 
 def screen_kernel(
@@ -251,7 +267,7 @@
     phases_ref,
     table_ref,
     series_ref,
-    residual_ref,
+    live_ref,
     map_ref,
     pair_out,
     pair_in,
@@ -304,37 +320,25 @@
     for device in [partner] + [device for _, _, device in plane + column]:
         pl.semaphore_signal(barrier, inc=1, device_id=device, device_id_type=MESH)
 
+    loads[1].wait()
+    fill_table(angles_ref, table_ref)
     loads[0].wait()
-    loads[1].wait()
-    map_ref[...] = pseudo_inverse(incidence_ref[...], table_filler(angles_ref, table_ref))
-    epochs = (2.0 * iota((DATES, 1), 0).astype(F32) - (DATES - 1)) / (DATES - 1)
-    spread = sum(((2.0 * n - (DATES - 1)) / (DATES - 1)) ** 2 for n in range(DATES))
+    design_t = design_rows(incidence_ref[...])
     for load in loads[2:]:
         load.wait()
 
     for tile in range(COL_DEV // TILE):
         cols = slice(tile * TILE, tile * TILE + TILE)
-        series = dot(map_ref[...], phases_ref[:, cols])
-        series_ref[:, cols] = series
-        offset = jnp.sum(series, axis=0, keepdims=True) / DATES
-        rate = jnp.sum(epochs * series, axis=0, keepdims=True) / spread
-        trend_ref[0, :, cols] = offset
-        trend_ref[1, :, cols] = rate
         live = coherent_ref[:, cols].astype(F32)
-        residual_ref[:, cols] = (live * (series - offset - epochs * rate)).astype(BF16)
-
-    def half_rows(half):
-        return pl.ds(pl.multiple_of(half * HALF, HALF), HALF)
-
-    def block(array, number):
-        row, col = number // 4 * 32, number % 4 * 128
-        return array[row : row + 32, col : col + 128]
+        live_ref[0, :, cols], live_ref[1, :, cols] = split(live * dot(design_t, phases_ref[:, cols]))
+
+    def spectrum(half):
+        table = table_ref[pl.ds(pl.multiple_of(half * FREQS, FREQS), FREQS), :]
+        return dot_nt(table, live_ref[1]) + dot_nt(table, live_ref[0])
 
     pl.semaphore_wait(barrier, 1 + len(plane) + len(column))
 
-    theirs = dot_nt(residual_ref[half_rows(1 - section), :], table_ref[...]).astype(BF16)
-    for number in range(PLANE):
-        pair_out[number] = block(theirs, number)
+    pair_out[...] = spectrum(1 - section)
     give = pltpu.make_async_remote_copy(
         src_ref=pair_out,
         dst_ref=pair_in,
@@ -344,10 +348,9 @@
         device_id_type=MESH,
     )
     give.start()
-    ours = dot_nt(residual_ref[half_rows(section), :], table_ref[...])
+    ours = spectrum(section)
     give.wait_recv()
-    for number in range(PLANE):
-        part_out[number] = (block(ours, number) + pair_in[number].astype(F32)).astype(BF16)
+    part_out[...] = (ours + pair_in[...]).reshape(PLANE, 16, DATES)
 
     def exchange(phase, mine, partners, source, target):
         for other, row, device in partners:
@@ -366,19 +369,43 @@
         pltpu.make_async_copy(blocks, blocks, sems.at[phase]).wait()
 
     exchange(0, me, plane, lambda other, row: part_out.at[other], part_in)
-    smooth = smooth_ref[...]
-    smooth_high = smooth.astype(BF16)
-    smooth_low = (smooth - smooth_high.astype(F32)).astype(BF16)
-    regroup, ungroup = regroup_matrix(False), regroup_matrix(True)
+    inverting = pseudo_inverse(incidence_ref[...], design_t)
+    regroup = regroup_matrix()
+    next(inverting)
+    next(inverting)
     arrived(0, part_in, recv_sems)
-    row_sum = jnp.sum(part_in[...].astype(F32).reshape(2, 256, 128), axis=0).astype(BF16)
-    up_out[...] = dot(regroup, row_sum).astype(BF16).reshape(DEPTH, 16, 128)
+    row_sum = jnp.sum(part_in[...].reshape(2, 128, DATES), axis=0)
+    terms = jnp.concatenate(split_fully(row_sum), axis=0)
+    rows = dot(jnp.concatenate([regroup, regroup, regroup], axis=1), terms)
+    up_out[...] = rows.reshape(DEPTH, SHELF, DATES)
     exchange(1, z, column, lambda other, row: up_out.at[other], up_in)
+    steps = list(inverting)
+    map_ref[...], total, final = steps[-1]
+    epochs = (2.0 * iota((DATES, 1), 0).astype(F32) - (DATES - 1)) / (DATES - 1)
+    epochs_row = (2.0 * iota((1, DATES), 1).astype(F32) - (DATES - 1)) / (DATES - 1)
+    spread = sum(((2.0 * n - (DATES - 1)) / (DATES - 1)) ** 2 for n in range(DATES))
     arrived(1, up_in, recv_sems)
-    rows = up_in[...].reshape(256, 128)
-    smoothed = dot(smooth_high, rows) + dot(smooth_low, rows)
-    down_out[...] = (smoothed * scale_ref[me % 2]).astype(BF16).reshape(DEPTH, 16, 128)
+    rows = dot_nt_fully(dot_nt_fully(up_in[...].reshape(128, DATES), total), final)
+    offset = jnp.sum(rows, axis=1, keepdims=True) / DATES
+    rate = jnp.sum(rows * epochs_row, axis=1, keepdims=True) / spread
+    rows = rows - offset - rate * epochs_row
+    smoothed = dot_split(split(smooth_ref[...]), split(rows))
+    scale = scale_ref[me * 16 + z]
+    halves = [
+        (smoothed[:, first : first + 128] * scale).reshape(DEPTH, SHELF, 128)
+        for first in (0, 128)
+    ]
+    down_out[...] = jnp.concatenate(halves, axis=1).astype(BF16)
     exchange(2, z, column, lambda other, row: down_out.at[other], down_in)
+
+    for tile in range(COL_DEV // TILE):
+        cols = slice(tile * TILE, tile * TILE + TILE)
+        series = dot(map_ref[...], phases_ref[:, cols])
+        series_ref[:, cols] = series
+        trend_ref[0, :, cols] = jnp.sum(series, axis=0, keepdims=True) / DATES
+        trend_ref[1, :, cols] = jnp.sum(epochs * series, axis=0, keepdims=True) / spread
+
+    ungroup = ungroup_matrix()
     arrived(2, down_in, recv_sems)
     whole = down_in[...].reshape(256, 128)
     back_out[...] = dot(ungroup, whole).astype(BF16).reshape(SHELF, 32, 128)
@@ -395,25 +422,29 @@
     )
     swap.start()
 
-    def correct(half, weights):
+    def keep(half, weights):
         for number in range(PLANE):
-            row, col = number // 4 * 32, number % 4 * 128
-            flat_ref[row : row + 32, col : col + 128] = weights[number]
-        dates = half_rows(half)
-        for tile in range(COL_DEV // TILE):
-            cols = slice(tile * TILE, tile * TILE + TILE)
-            screen = dot(flat_ref[...], table_ref[:, cols]).astype(BF16).astype(F32)
-            live = coherent_ref[:, cols].astype(F32)
-            corrected_ref[dates, cols] = (live * (series_ref[dates, cols] - screen)).astype(BF16)
-
-    correct(section, back_in)
+            first = pl.multiple_of(half * FREQS + number * 16, 16)
+            for dates in (0, 1):
+                flat_ref[pl.ds(first, 16), dates * 128 : dates * 128 + 128] = weights[
+                    number, dates * 16 : dates * 16 + 16
+                ]
+
+    keep(section, back_in)
     give.wait_send()
     arrived(0, part_in, send_sems)
     arrived(1, up_in, send_sems)
     arrived(2, down_in, send_sems)
     arrived(3, back_in, send_sems)
     swap.wait_recv()
-    correct(1 - section, swap_in)
+    keep(1 - section, swap_in)
+    eye = hot(iota((DATES, DATES), 0) == iota((DATES, DATES), 1)).astype(BF16)
+    weights = dot_nt(eye, flat_ref[...]).astype(BF16)
+    for tile in range(COL_DEV // TILE):
+        cols = slice(tile * TILE, tile * TILE + TILE)
+        screen = dot(weights, table_ref[:, cols]).astype(BF16).astype(F32)
+        live = coherent_ref[:, cols].astype(F32)
+        corrected_ref[:, cols] = (live * (series_ref[:, cols] - screen)).astype(BF16)
     swap.wait_send()
 
 
@@ -453,25 +484,25 @@
             pltpu.VMEM((2, ifgs), jnp.int32),
             pltpu.VMEM((1, COL_DEV), jnp.int32),
             pltpu.VMEM((4, FREQS, 128), F32),
-            pltpu.VMEM((256, 256), F32),
-            pltpu.VMEM((2, 1, 128), F32),
+            pltpu.VMEM((128, 128), F32),
+            pltpu.VMEM((FREQS, 1, 128), F32),
             pltpu.VMEM((ifgs, COL_DEV), BF16),
             pltpu.VMEM((2 * FREQS, COL_DEV), BF16),
             pltpu.VMEM((DATES, COL_DEV), F32),
-            pltpu.VMEM((DATES, COL_DEV), BF16),
+            pltpu.VMEM((2, DATES, COL_DEV), BF16),
             pltpu.VMEM((DATES, ifgs), BF16),
-            pltpu.VMEM((PLANE, 32, 128), BF16),
-            pltpu.VMEM((PLANE, 32, 128), BF16),
-            pltpu.VMEM((PLANE, 32, 128), BF16),
-            pltpu.VMEM((PLANE, 32, 128), BF16),
-            pltpu.VMEM((DEPTH, 16, 128), BF16),
-            pltpu.VMEM((DEPTH, 16, 128), BF16),
+            pltpu.VMEM((FREQS, DATES), F32),
+            pltpu.VMEM((FREQS, DATES), F32),
+            pltpu.VMEM((PLANE, 16, DATES), F32),
+            pltpu.VMEM((PLANE, 16, DATES), F32),
+            pltpu.VMEM((DEPTH, SHELF, DATES), F32),
+            pltpu.VMEM((DEPTH, SHELF, DATES), F32),
             pltpu.VMEM((DEPTH, 16, 128), BF16),
             pltpu.VMEM((DEPTH, 16, 128), BF16),
             pltpu.VMEM((SHELF, 32, 128), BF16),
             pltpu.VMEM((PLANE, 32, 128), BF16),
             pltpu.VMEM((PLANE, 32, 128), BF16),
-            pltpu.VMEM((HALF, 2 * FREQS), BF16),
+            pltpu.VMEM((2 * FREQS, DATES), BF16),
             pltpu.SemaphoreType.DMA((6,)),
             pltpu.SemaphoreType.DMA((6,)),
             pltpu.SemaphoreType.DMA((6,)),

time: 47.8 us -> 54.7 us (1.14)
  Pallas kernels: 47 us -> 53.9 us
    pallas_call x1, Pallas kernels: 46 us -> 52.9 us  [per_device(): pl.pallas_call(screen_kernel, out_shape=results, in_specs=[in_hbm] * 6, o...]
where the time goes in v7:
time: 54.7 us; the launch traced here: 54.6 us
  Pallas kernels  53.9 us (99%)
  between operations  0.64 us (1%)
    pallas_call x1, Pallas kernels, per_device(): pl.pallas_call(screen_kernel, out_shape=results, in_specs=[in_hbm] * 6, o...  52.9 us

profile of v7, /device:TPU:1, one launch (start us, length us, event | category | flops | bytes accessed | tf_op | source)
XLA Modules:
  0.0 54.6 jit_solution(1725254855600424518)
XLA Ops:
  0.6 52.9 %screen.1 = (bf16[256,2048]{1,0:T(8,128)(2,1)S(1)}, f32[2,1,2048]{2,1,0:T(1,128)S(1)}) custom-call(s32[2,600]{1,0:T(2,128)} %bitcast.4, s32[1,2048]{1,0:T(1,128)} %coherent_hbm.1, f32[4,256,128]{2,1,0:T(8,128)} %constant.6.clone.angles_hbm, f32[128,128]{1,0:T(8,128)} %constant.7.clone.smooth_hbm, f32[256,1,128]{2,1,0:T(1,128)} %constant.8.clone.scale_hbm, ...), custom_call_target="tpu_custom_call" | custom-call | tf_op jit(solution)/shard_map/screen/pallas_call | solution.py:478
  53.6 1.0 %store.1 = (bf16[256,2048]{1,0:T(8,128)(2,1)}, f32[2,1,2048]{2,1,0:T(1,128)}) custom-call(bf16[256,2048]{1,0:T(8,128)(2,1)S(1)} %get-tuple-element.6.corrected_ref, f32[2,1,2048]{2,1,0:T(1,128)S(1)} %get-tuple-element.7.trend_ref), custom_call_target="tpu_custom_call" | custom-call | tf_op jit(solution)/shard_map/store/pallas_call | solution.py:515
